TPU v7x, 256 devices: a whole 4x4x8 slice. The times are simulated.
256 devices in a mesh: orb: 64 (over x, z, core), box: 4 (over y).
Axes of the slice: x: 4, y: 4, z: 8, core: 2. Of those that a mesh axis runs over, the one named last changes fastest.
Arguments:
- psi: float32 [512, 64, 4096], P('orb', 'box'), may hold values from -6 to 6
- potential: float32 [64, 4096], P('box'), may hold values from -3 to 3
- orbital_slot: int32 [256], replicated, may hold values from 0 to 511, as said below
Outputs:
- residual: float32 [256, 64, 4096], P('orb', 'box')
- direction: float32 [256, 64, 4096], P('orb', 'box')
- multipliers: float32 [256, 256], replicated
Inputs may be any that keep to these rules, and one draw needn't show every extreme that they name: The values are distinct slots: orbital j sits in slot orbital_slot[j]. The 8 slots of one index of orb hold up to 8 orbitals, and in every draw all slots of one index are filled.
All inputs are finite; a program needn't handle non-finite values.
Results may differ from a plain program's by a relative error of at most 0.0002.
Values sent between devices are 32-bit elements; how exact they have to be, the bound alone decides.
A program may use at most 64 MiB of HBM per device.

v0:
```python
import math

import jax
import jax.numpy as jnp
import numpy as np
from jax import lax
from jax.sharding import PartitionSpec as P

MTAPS = 16
KREACH = 14
SWEEPS = 4


highest = lax.Precision.HIGHEST
coupling_z = 4.0
coupling_xy = 1.0


def extended_2(block, sides, width):
    for axis, dim in sides:
        count = lax.axis_size(axis)
        forward = [(i, i + 1) for i in range(count - 1)]
        backward = [(target, source) for source, target in forward]
        low = lax.ppermute(
            lax.slice_in_dim(block, block.shape[dim] - width, None, axis=dim), axis, forward
        )
        high = lax.ppermute(lax.slice_in_dim(block, 0, width, axis=dim), axis, backward)
        block = jnp.concatenate([low, block, high], axis=dim)
    return block


def magic_weights(tap_count):
    half_len = tap_count // 2
    offsets = np.arange(1 - half_len, half_len + 1) * 1.0
    weights = np.ones(tap_count)
    for index_a in range(tap_count):
        for index_b in range(tap_count):
            if index_b != index_a:
                weights[index_a] *= (0.25 - offsets[index_b]) / (
                    offsets[index_a] - offsets[index_b]
                )
    return weights


def second_weights(reach_cells):
    factor = math.factorial(reach_cells) ** 2
    weights = np.zeros(2 * reach_cells + 1)
    for distance in range(1, reach_cells + 1):
        entry_value = (
            2.0
            * (-1) ** (distance + 1)
            * factor
            / (
                distance
                * distance
                * math.factorial(reach_cells - distance)
                * math.factorial(reach_cells + distance)
            )
        )
        weights[reach_cells + distance] = entry_value
        weights[reach_cells - distance] = entry_value
    weights[reach_cells] = -weights.sum()
    return -0.5 * weights


def banded(row_count, col_count, row_start, col_start, weights, offset_low):
    row_index = np.arange(row_count)[:, None] + row_start
    col_index = np.arange(col_count)[None, :] + col_start
    position = row_index - col_index - offset_low
    inside = (position >= 0) & (position < len(weights))
    return np.where(inside, weights[np.clip(position, 0, len(weights) - 1)], 0.0)


def along_cols(values, matrix, box_width):
    repeats = max(1, 128 // box_width)
    blocked = jnp.asarray(np.kron(np.eye(repeats), matrix), dtype=jnp.float32)
    shaped = values.shape
    result = jnp.dot(values.reshape(-1, box_width * repeats), blocked, precision=highest)
    return result.reshape(shaped)


def along_rows(values, matrix, box_width):
    shaped = values.shape
    split_rows = values.reshape(shaped[:-1] + (box_width, box_width))
    result = jnp.einsum(
        "nzyx,yq->nzqx", split_rows, jnp.asarray(matrix, dtype=jnp.float32), precision=highest
    )
    return result.reshape(shaped)


def apply_hamiltonian(coeffs, potential, box_width):
    count, slab_depth, plane_size = coeffs.shape
    margin = MTAPS
    half_len = MTAPS // 2
    stacked = jnp.concatenate([coeffs, potential[None]], 0)
    extended = extended_2(stacked, (("box", 1),), margin)
    coeff_ext = extended[:count]
    potential_ext = extended[count]
    magic = magic_weights(MTAPS)
    kinetic_row = second_weights(KREACH)
    into_grid = jnp.asarray(
        banded(
            slab_depth + 2 * margin,
            slab_depth + 2 * half_len,
            -margin,
            -half_len,
            magic,
            1 - half_len,
        ),
        dtype=jnp.float32,
    )
    from_grid = jnp.asarray(
        banded(slab_depth, slab_depth + 2 * half_len, 0, -half_len, magic, 1 - half_len).T,
        dtype=jnp.float32,
    )
    kinetic_z = jnp.asarray(
        banded(slab_depth + 2 * margin, slab_depth, -margin, 0, kinetic_row, -KREACH),
        dtype=jnp.float32,
    )
    forward = banded(box_width, box_width, 0, 0, magic, 1 - half_len)
    kinetic_xy = banded(box_width, box_width, 0, 0, kinetic_row, -KREACH)
    grid_values = jnp.einsum("nea,ep->npa", coeff_ext, into_grid, precision=highest)
    grid_values = along_cols(along_rows(grid_values, forward, box_width), forward, box_width)
    potential_slab = potential_ext[margin - half_len : margin + slab_depth + half_len]
    weighted = grid_values * potential_slab[None]
    weighted = along_cols(
        along_rows(weighted, forward.T.copy(), box_width), forward.T.copy(), box_width
    )
    applied = jnp.einsum("npa,pz->nza", weighted, from_grid, precision=highest)
    local_part = coeff_ext[:, margin : margin + slab_depth]
    applied = applied + along_rows(local_part, kinetic_xy, box_width)
    applied = applied + along_cols(local_part, kinetic_xy, box_width)
    applied = applied + jnp.einsum("nea,ez->nza", coeff_ext, kinetic_z, precision=highest)
    return applied


def relax(iterate, residual, denominator, box_width):
    count, slab_depth, plane_size = iterate.shape
    extended = extended_2(iterate, (("box", 1),), 1)
    along_z = extended[:, :-2] + extended[:, 2:]
    column = lax.broadcasted_iota(jnp.int32, (1, 1, plane_size), 2) % box_width
    zero_col = jnp.zeros((count, slab_depth, 1), jnp.float32)
    zero_row = jnp.zeros((count, slab_depth, box_width), jnp.float32)
    left_side = jnp.concatenate([zero_col, iterate[..., :-1]], 2) * (column != 0).astype(
        jnp.float32
    )
    right_side = jnp.concatenate([iterate[..., 1:], zero_col], 2) * (
        column != box_width - 1
    ).astype(jnp.float32)
    upper_row = jnp.concatenate([zero_row, iterate[..., :-box_width]], 2)
    lower_row = jnp.concatenate([iterate[..., box_width:], zero_row], 2)
    beside = left_side + right_side + upper_row + lower_row
    return (residual + coupling_xy * beside + coupling_z * along_z) / denominator


def local(psi, potential, orbital_slot):
    slot_count, slab_depth, plane_size = psi.shape
    box_width = math.isqrt(plane_size)
    flattened = psi.reshape(slot_count, slab_depth * plane_size)
    pieces = lax.all_to_all(flattened, "orb", split_axis=1, concat_axis=0, tiled=True)
    coeff_rows = jnp.take(pieces, orbital_slot, axis=0)
    owned_rows = lax.all_to_all(coeff_rows, "orb", split_axis=0, concat_axis=1, tiled=True)
    own_count = owned_rows.shape[0]
    applied = apply_hamiltonian(
        owned_rows.reshape(own_count, slab_depth, plane_size), potential, box_width
    )
    applied_rows = lax.all_to_all(
        applied.reshape(own_count, slab_depth * plane_size),
        "orb",
        split_axis=1,
        concat_axis=0,
        tiled=True,
    )
    partial_value = jnp.einsum("ia,ja->ij", coeff_rows, applied_rows, precision=highest) / float(
        box_width**3
    )
    multipliers = lax.psum(partial_value, ("orb", "box"))
    corrected = applied_rows - jnp.einsum("ji,ja->ia", multipliers, coeff_rows, precision=highest)
    returned = lax.all_to_all(corrected, "orb", split_axis=0, concat_axis=1, tiled=True)
    own_count = returned.shape[0]
    residual = returned.reshape(own_count, slab_depth, plane_size)
    first_row = lax.axis_index("orb") * own_count
    own_diagonal = lax.dynamic_slice_in_dim(jnp.diagonal(multipliers), first_row, own_count)
    denominator = (2.0 * coupling_z + 4.0 * coupling_xy + 1.0 + jnp.abs(own_diagonal))[
        :, None, None
    ]
    direction = residual / denominator
    for sweep_index in range(SWEEPS):
        direction = relax(direction, residual, denominator, box_width)
    return (residual, direction, multipliers)


def solution(mesh):
    in_specs = (P("orb", "box", None), P("box", None), P())
    out_specs = (P("orb", "box", None), P("orb", "box", None), P())
    return jax.shard_map(local, mesh=mesh, in_specs=in_specs, out_specs=out_specs, check_vma=False)
```

profile of v0, /device:TPU:2, one launch (start us, length us, event | category | flops | bytes accessed | tf_op | source)
XLA Modules:
  0.0 610.0 jit_solution(12375288629331391101)
XLA Ops:
  7.2 1.9 all_to_all.50
  9.1 2.6 copy.47
  11.6 12.2 %all-to-all-start = ((f32[8,64,1024]{2,0,1:T(8,128)}), f32[8,64,1024]{2,0,1:T(8,128)S(1)}, u32[]{:S(2)}, u32[]{:S(2)}) async-start(f32[8,64,1024]{2,0,1:T(8,128)} %copy.47), calls=%async_computation | async-start | bytes 4194304 | tf_op jit(solution)/shard_map/all_to_all | solution.py:160
  24.0 49.3 %all-to-all-done = f32[8,64,1024]{2,0,1:T(8,128)S(1)} async-done(((f32[8,64,1024]{2,0,1:T(8,128)}), f32[8,64,1024]{2,0,1:T(8,128)S(1)}, u32[]{:S(2)}, u32[]{:S(2)}) %all-to-all-start) | async-done | bytes 2097184 | tf_op jit(solution)/shard_map/all_to_all | solution.py:160
  75.0 34.5 %all_to_all.67 = f32[64,4,1024]{2,1,0:T(4,128)S(1)} all-to-all(f32[64,4,1024]{2,1,0:T(4,128)S(1)} %broadcast_select_fusion), channel_id=1, replica_groups=mesh['orb'=64,'box'=4] {'orb'}, dimensions={0} | all-to-all | bytes 2097152 | tf_op jit(solution)/shard_map/all_to_all | solution.py:162
  111.8 4.7 collective-permute-start
  117.7 1.9 reshape.99
  120.8 6.4 %convolution_bitcast_fusion.4 = f32[4,16,64,64]{2,3,1,0:T(8,128)} fusion(f32[4,16,64,64]{3,2,1,0:T(8,128)} %reshape.99, f32[64,64,1,1]{1,0,3,2:T(8,128)S(1)} %copy-done.8), kind=kOutput, calls=%fused_computation.14 | convolution fusion | flops 201326592 | bytes 2113536 | tf_op jit(solution)/shard_map/nzyx,yq->nzqx/dot_general | solution.py:85
  127.1 3.4 copy.56
  130.5 2.2 reshape.100
  132.7 3.2 fusion.56
  135.9 2.4 reshape.102
  138.3 6.2 %collective-permute-done = f32[5,16,4096]{2,1,0:T(8,128)} collective-permute-done((f32[5,16,4096]{2,1,0:T(8,128)}, f32[5,16,4096]{2,1,0:T(8,128)}, u32[]{:S(2)}, u32[]{:S(2)}) %collective-permute-start) | collective-permute-done | bytes 1310752 | tf_op jit(solution)/shard_map/ppermute | solution.py:24
  144.5 5.6 collective-permute-done.1
  150.1 5.1 convolution_bitcast_fusion
  155.2 4.6 reshape.96
  159.9 9.9 %convolution_bitcast_fusion.3 = f32[4,32,64,64]{2,3,1,0:T(8,128)} fusion(f32[4,32,64,64]{3,2,1,0:T(8,128)} %reshape.96, f32[64,64,1,1]{1,0,3,2:T(8,128)S(1)} %copy-done.7), kind=kOutput, calls=%fused_computation.12 | convolution fusion | flops 402653184 | bytes 4210688 | tf_op jit(solution)/shard_map/nzyx,yq->nzqx/dot_general | solution.py:85
  169.7 5.7 copy.50
  175.4 4.7 reshape_reshape.6
  180.1 4.7 fusion.54
  184.8 4.6 reshape.97
  189.4 5.7 copy.52
  195.0 1.8 pad_maximum_fusion.12
  196.8 2.4 mul.90
  199.3 2.6 copy.51
  201.8 6.7 %fusion.5 = f32[4,32,64,64]{2,3,1,0:T(8,128)} fusion(f32[64,64,1,1]{1,0,3,2:T(8,128)S(1)} %copy-done.6, f32[4,32,64,64]{2,3,1,0:T(8,128)} %copy.52, f32[32,64,64]{1,2,0:T(8,128)} %copy.51), kind=kOutput, calls=%fused_computation.11 | convolution fusion | flops 403177472 | bytes 4734976 | tf_op jit(solution)/shard_map/nzyx,yq->nzqx/dot_general | solution.py:85
  208.5 5.7 copy.53
  214.2 4.7 reshape_reshape.7
  218.8 4.7 fusion.55
  223.6 2.8 reshape.98
  226.3 3.2 fusion.2
  229.5 4.3 fusion
  236.0 33.6 %all_to_all.68 = f32[4,64,1024]{2,0,1:T(4,128)S(1)} all-to-all(f32[4,64,1024]{2,0,1:T(4,128)S(1)} %copy.58), channel_id=1, replica_groups=mesh['orb'=64,'box'=4] {'orb'}, dimensions={1} | all-to-all | bytes 2097152 | tf_op jit(solution)/shard_map/all_to_all | solution.py:167
  270.0 1.8 convolution_multiply_fusion
  271.8 247.7 %all-reduce.18.cloned.1.call-done = f32[256,256]{1,0:T(8,128)} async-done(((f32[256,256]{1,0:T(8,128)}), f32[256,256]{1,0:T(8,128)}) %all-reduce.18.cloned.1.call-update) | async-done | bytes 262160 | tf_op jit(solution)/shard_map/psum | solution.py:177
  519.5 2.1 convolution_subtract_fusion
  522.9 8.6 %all-to-all-start.3 = ((f32[64,4,1024]{2,1,0:T(4,128)}), f32[64,4,1024]{2,1,0:T(4,128)S(1)}, u32[]{:S(2)}, u32[]{:S(2)}) async-start(f32[64,4,1024]{2,1,0:T(4,128)} %all_to_all.60), calls=%async_computation.3 | async-start | bytes 2097152 | tf_op jit(solution)/shard_map/all_to_all | solution.py:179
  531.6 2.3 gather_fusion.1
  534.0 24.7 %all-to-all-done.3 = f32[64,4,1024]{2,1,0:T(4,128)S(1)} async-done(((f32[64,4,1024]{2,1,0:T(4,128)}), f32[64,4,1024]{2,1,0:T(4,128)S(1)}, u32[]{:S(2)}, u32[]{:S(2)}) %all-to-all-start.3) | async-done | bytes 1048608 | tf_op jit(solution)/shard_map/all_to_all | solution.py:179
  560.4 2.7 collective-permute-start.2
  565.2 4.6 collective-permute-done.3
  571.0 3.4 collective-permute-start.4
  576.3 4.3 collective-permute-done.5
  581.8 3.1 collective-permute-start.6
  586.9 4.3 collective-permute-done.7
  592.4 1.9 collective-permute-start.8
  596.2 4.3 collective-permute-done.9
  600.5 1.8 fusion.12
  (74 shorter events, 24.3 us)
Async XLA Ops:
  11.6 12.2 %copy-start.10 = (s32[256]{0:T(256)S(1)}, s32[256]{0:T(256)}, u32[]{:S(2)}) copy-start(s32[256]{0:T(256)} %param.14) | copy-start | bytes 3076
  11.6 61.7 %all-to-all-start = ((f32[8,64,1024]{2,0,1:T(8,128)}), f32[8,64,1024]{2,0,1:T(8,128)S(1)}, u32[]{:S(2)}, u32[]{:S(2)}) async-start(f32[8,64,1024]{2,0,1:T(8,128)} %copy.47), calls=%async_computation | async-start | bytes 4194304 | tf_op jit(solution)/shard_map/all_to_all | solution.py:160
  23.8 495.7 %all-reduce.18.cloned.1.call-start = ((), (), s32[]{:S(2)}) async-start(), calls=%async_computation.4 | async-start | bytes 524288 | tf_op jit(solution)/shard_map/psum | solution.py:177
  109.5 1.1 copy-start.2
  111.8 9.0 %copy-start.8 = (f32[64,64,1,1]{1,0,3,2:T(8,128)S(1)}, f32[64,64,1,1]{1,0,3,2:T(8,128)}, u32[]{:S(2)}) copy-start(f32[64,64,1,1]{1,0,3,2:T(8,128)} %constant.145) | copy-start | bytes 49156
  111.8 32.7 %collective-permute-start = (f32[5,16,4096]{2,1,0:T(8,128)}, f32[5,16,4096]{2,1,0:T(8,128)}, u32[]{:S(2)}, u32[]{:S(2)}) collective-permute-start(f32[5,16,4096]{2,1,0:T(8,128)} %pad_maximum_fusion.3), channel_id=1, source_target_pairs={{0,1},{1,2},{2,3},{4,5},{5,6},{6,7},{8,9},{9,10},{10,11},{12,13},{... | collective-permute-start | bytes 3932168 | tf_op jit(solution)/shard_map/ppermute | solution.py:24
  116.4 33.7 %collective-permute-start.1 = (f32[5,16,4096]{2,1,0:T(8,128)}, f32[5,16,4096]{2,1,0:T(8,128)}, u32[]{:S(2)}, u32[]{:S(2)}) collective-permute-start(f32[5,16,4096]{2,1,0:T(8,128)} %pad_maximum_fusion.3), channel_id=1, source_target_pairs={{1,0},{2,1},{3,2},{5,4},{6,5},{7,6},{9,8},{10,9},{11,10},{13,12},{... | collective-permute-start | bytes 3932168 | tf_op jit(solution)/shard_map/ppermute | solution.py:27
  130.5 2.2 copy-start.5
  132.7 17.5 %copy-start.11 = (f32[48,32,1]{0,1,2:T(8,128)S(1)}, f32[48,32,1]{0,1,2:T(8,128)}, u32[]{:S(2)}) copy-start(f32[48,32,1]{0,1,2:T(8,128)} %constant.141) | copy-start | bytes 18436
  155.2 4.7 copy-start.7
  175.4 4.7 copy-start.4
  196.8 5.0 copy-start.6
  214.2 4.7 copy-start.3
  223.6 2.8 copy-start.9
  226.3 3.2 copy-start.12
  521.6 9.9 %copy-start.1 = (f32[256,256]{1,0:T(8,128)S(1)}, f32[256,256]{1,0:T(8,128)}, u32[]{:S(2)}) copy-start(f32[256,256]{1,0:T(8,128)} %all-reduce.18.cloned.1.call-done) | copy-start | bytes 786436
  522.9 35.8 %all-to-all-start.3 = ((f32[64,4,1024]{2,1,0:T(4,128)}), f32[64,4,1024]{2,1,0:T(4,128)S(1)}, u32[]{:S(2)}, u32[]{:S(2)}) async-start(f32[64,4,1024]{2,1,0:T(4,128)} %all_to_all.60), calls=%async_computation.3 | async-start | bytes 2097152 | tf_op jit(solution)/shard_map/all_to_all | solution.py:179
  559.8 40.7 %copy-start = (f32[4,16,4096]{2,1,0:T(8,128)}, f32[4,16,4096]{2,1,0:T(8,128)S(1)}, u32[]{:S(2)}) copy-start(f32[4,16,4096]{2,1,0:T(8,128)S(1)} %reshape.103) | copy-start | bytes 3145732
  560.4 4.8 collective-permute-start.2
  563.1 6.7 %collective-permute-start.3 = (f32[4,1,4096]{2,1,0:T(1,128)S(1)}, f32[4,1,4096]{2,1,0:T(1,128)S(1)}, u32[]{:S(2)}, u32[]{:S(2)}) collective-permute-start(f32[4,1,4096]{2,1,0:T(1,128)S(1)} %get-tuple-element.26), channel_id=1, source_target_pairs={{1,0},{2,1},{3,2},{5,4},{6,5},{7,6},{9,8},{10,9},{11,10},{13,12},{... | collective-permute-start | bytes 196616 | tf_op jit(solution)/shard_map/ppermute | solution.py:27
  571.0 5.3 collective-permute-start.4
  574.4 6.2 %collective-permute-start.5 = (f32[4,1,4096]{2,1,0:T(1,128)S(1)}, f32[4,1,4096]{2,1,0:T(1,128)S(1)}, u32[]{:S(2)}, u32[]{:S(2)}) collective-permute-start(f32[4,1,4096]{2,1,0:T(1,128)S(1)} %get-tuple-element.20), channel_id=1, source_target_pairs={{1,0},{2,1},{3,2},{5,4},{6,5},{7,6},{9,8},{10,9},{11,10},{13,12},{... | collective-permute-start | bytes 196616 | tf_op jit(solution)/shard_map/ppermute | solution.py:27
  581.8 5.0 collective-permute-start.6
  585.0 6.2 %collective-permute-start.7 = (f32[4,1,4096]{2,1,0:T(1,128)S(1)}, f32[4,1,4096]{2,1,0:T(1,128)S(1)}, u32[]{:S(2)}, u32[]{:S(2)}) collective-permute-start(f32[4,1,4096]{2,1,0:T(1,128)S(1)} %get-tuple-element.14), channel_id=1, source_target_pairs={{1,0},{2,1},{3,2},{5,4},{6,5},{7,6},{9,8},{10,9},{11,10},{13,12},{... | collective-permute-start | bytes 196616 | tf_op jit(solution)/shard_map/ppermute | solution.py:27
  592.4 3.8 collective-permute-start.8
  594.3 6.2 %collective-permute-start.9 = (f32[4,1,4096]{2,1,0:T(1,128)S(1)}, f32[4,1,4096]{2,1,0:T(1,128)S(1)}, u32[]{:S(2)}, u32[]{:S(2)}) collective-permute-start(f32[4,1,4096]{2,1,0:T(1,128)S(1)} %get-tuple-element.8), channel_id=1, source_target_pairs={{1,0},{2,1},{3,2},{5,4},{6,5},{7,6},{9,8},{10,9},{11,10},{13,12},{... | collective-permute-start | bytes 196616 | tf_op jit(solution)/shard_map/ppermute | solution.py:27
Sparse Core Ops, SparseCore 0:
  271.9 247.5 all-reduce.17
where the time goes:
time: 619 us; the launch traced here: 610 us
  waiting for transfers between devices  352 us (57%)
  local copies, waits for them, and re-layouts  72.4 us (12%)
  blocking collectives  68 us (11%)
  matrix products  52 us (8%)
  starting transfers between devices  43.1 us (7%)
  between operations  14.6 us (2%)
  other arithmetic  7.64 us (1%)
    psum x1, waiting for transfers between devices, local(): multipliers = lax.psum(partial_value, ('orb', 'box'))  248 us
    all_to_all x1, waiting for transfers between devices, local(): lax.all_to_all(flattened, 'orb', split_axis=1, concat_axis=0, tiled=True)  49.3 us
    all_to_all x1, blocking collectives, local(): lax.all_to_all(coeff_rows, 'orb', split_axis=0, concat_axis=1, tiled=True)  34.5 us
    all_to_all x1, blocking collectives, local(): lax.all_to_all(applied.reshape(own_count, slab_depth * plane_size), 'orb'...  33.6 us
    all_to_all x1, waiting for transfers between devices, local(): lax.all_to_all(corrected, 'orb', split_axis=0, concat_axis=1, tiled=True)  24.7 us
    ppermute x5, waiting for transfers between devices, extended_2(): lax.ppermute(lax.slice_in_dim(block, 0, width, axis=dim), axis, backward)  23.1 us
    dot_general x3, matrix products, along_rows(): jnp.einsum('nzyx,yq->nzqx', split_rows, jnp.asarray(matrix, dtype=jnp.flo...  22.9 us
    ppermute x5, starting transfers between devices, extended_2(): lax.ppermute(lax.slice_in_dim(block, block.shape[dim] - width, None, axis...  15.8 us
  transfers between devices with their start and end apart: 13, of which 13 were waited for; matrix products, arithmetic and copies ran while one was open for 4% of the time, Pallas kernels for 0%

commit v1 on v0

v1 whole, which is shorter than its diff:
```python
import math

import jax
import jax.numpy as jnp
import ml_dtypes
import numpy as np
from jax import lax
from jax.experimental import pallas as pl
from jax.experimental.pallas import tpu as pltpu
from jax.sharding import PartitionSpec as P

G = 64
MTAPS = 16
KREACH = 14
SWEEPS = 4
ORB, BOX = 64, 4
SLOTS, ORBS, OWN = 8, 256, 4
DEPTH = 16
PLANE = G * G
LANES = 256
TILES = PLANE // LANES
FPAD, KPAD = 2, 4

coupling_z = 4.0
coupling_xy = 1.0

F32, BF16 = jnp.float32, jnp.bfloat16
ANY = pl.BlockSpec(memory_space=pl.ANY)
VMEM = pl.BlockSpec(memory_space=pltpu.VMEM)
VLIMIT = 56 * 2**20


def magic_weights(tap_count):
    half_len = tap_count // 2
    offsets = np.arange(1 - half_len, half_len + 1) * 1.0
    weights = np.ones(tap_count)
    for index_a in range(tap_count):
        for index_b in range(tap_count):
            if index_b != index_a:
                weights[index_a] *= (0.25 - offsets[index_b]) / (
                    offsets[index_a] - offsets[index_b]
                )
    return weights


def second_weights(reach_cells):
    factor = math.factorial(reach_cells) ** 2
    weights = np.zeros(2 * reach_cells + 1)
    for distance in range(1, reach_cells + 1):
        entry_value = (
            2.0
            * (-1) ** (distance + 1)
            * factor
            / (
                distance
                * distance
                * math.factorial(reach_cells - distance)
                * math.factorial(reach_cells + distance)
            )
        )
        weights[reach_cells + distance] = entry_value
        weights[reach_cells - distance] = entry_value
    weights[reach_cells] = -weights.sum()
    return -0.5 * weights


def banded(row_count, col_count, row_start, col_start, weights, offset_low):
    row_index = np.arange(row_count)[:, None] + row_start
    col_index = np.arange(col_count)[None, :] + col_start
    position = row_index - col_index - offset_low
    inside = (position >= 0) & (position < len(weights))
    return np.where(inside, weights[np.clip(position, 0, len(weights) - 1)], 0.0)


def halves(table):
    table = np.asarray(table, np.float32)
    high = table.astype(ml_dtypes.bfloat16)
    low = (table - high.astype(np.float32)).astype(ml_dtypes.bfloat16)
    return high, low


def tables():
    magic = magic_weights(MTAPS)
    kinetic_row = second_weights(KREACH)
    forward = banded(G, G, 0, 0, magic, 1 - MTAPS // 2)
    kinetic = banded(G, G, 0, 0, kinetic_row, -KREACH)
    rows = LANES // G

    def beside(high, low):
        return np.concatenate([high, high, low], 1)

    z_in = beside(*halves(np.concatenate([forward.T, kinetic], 0)))
    z_out = beside(*halves(forward))
    into, back, kin = [], [], []
    for step in range(-FPAD, FPAD + 1):
        block = banded(rows, rows, rows * step, 0, magic, 1 - MTAPS // 2)
        into.append(np.kron(block, forward))
        block = banded(rows, rows, -rows * step, 0, magic, 1 - MTAPS // 2).T
        back.append(np.kron(block, forward.T))
    for step in range(-KPAD, KPAD + 1):
        block = np.kron(banded(rows, rows, rows * step, 0, kinetic_row, -KREACH), np.eye(G))
        if step == 0:
            block = block + np.kron(np.eye(rows), kinetic)
        kin.append(block)
    return [z_in, z_out] + [np.stack(halves(np.stack(m))) for m in (into, back, kin)]


def split(values):
    high = values.astype(BF16)
    return high, (values - high.astype(F32)).astype(BF16)


def mm(left, right):
    return jnp.dot(left, right, preferred_element_type=F32)


def place():
    orb = lax.axis_index("orb")
    box = lax.axis_index("box")
    return orb, box, orb // 16, (orb // 2) % 8, orb % 2


def shifted(orb, step):
    x, z, core = orb // 16, (orb // 2) % 8, orb % 2
    dx, dz, dc = step // 16, (step // 2) % 8, step % 2
    return ((x + dx) % 4) * 16 + ((z + dz) % 8) * 2 + (core + dc) % 2


def remote(src, dst, send, recv, orb, box):
    return pltpu.make_async_remote_copy(
        src_ref=src,
        dst_ref=dst,
        send_sem=send,
        recv_sem=recv,
        device_id={"orb": orb, "box": box},
        device_id_type=pl.DeviceIdType.MESH,
    )


def wait_for(ref, sem):
    pltpu.make_async_copy(ref, ref, sem).wait()


def tile_of(orb):
    return pl.ds(pl.multiple_of((orb // 32) * 8, 8), 8), pl.ds(
        pl.multiple_of((orb % 32) * 128, 128), 128
    )


def exchange_kernel(psi, pot, pieces, cube, vfull, own, p_send, p_recv, y_send, y_recv, v_send, v_recv):
    orb, box, _, _, _ = place()
    slab = pl.ds(pl.multiple_of(box * DEPTH, DEPTH), DEPTH)
    for step in range(1, BOX):
        to = (box + step) % BOX
        remote(psi.at[pl.ds(2 * to, 2)], cube.at[:, slab, :], y_send, y_recv, orb, to).start()
        remote(pot, vfull.at[slab, :], v_send, v_recv, orb, to).start()
    mine = pltpu.make_async_copy(psi.at[pl.ds(2 * box, 2)], cube.at[:, slab, :], own.at[0])
    mine.start()
    vmine = pltpu.make_async_copy(pot, vfull.at[slab, :], own.at[1])
    vmine.start()
    target = pl.ds(pl.multiple_of(orb * SLOTS, SLOTS), SLOTS)
    z_rows, lanes = tile_of(orb)
    pmine = pltpu.make_async_copy(psi.at[:, z_rows, lanes], pieces.at[target], own.at[2])
    pmine.start()

    def send(step, carry):
        to = shifted(orb, step)
        z_rows, lanes = tile_of(to)
        remote(psi.at[:, z_rows, lanes], pieces.at[target], p_send, p_recv, to, box).start()
        return carry

    lax.fori_loop(1, ORB, send, 0)
    mine.wait()
    vmine.wait()
    pmine.wait()
    third = cube.at[:, pl.ds(0, 3 * DEPTH), :]
    wait_for(third, y_send)
    wait_for(third, y_recv)
    wait_for(vfull.at[pl.ds(0, 3 * DEPTH)], v_send)
    wait_for(vfull.at[pl.ds(0, 3 * DEPTH)], v_recv)
    wait_for(pieces.at[pl.ds(0, SLOTS * (ORB - 1))], p_send)
    wait_for(pieces.at[pl.ds(0, SLOTS * (ORB - 1))], p_recv)


def apply_kernel(cube, vfull, z_in, z_out, into, back, kin, out, c_hi, c_lo, t_hi, t_lo, s_hi, s_lo, kz):
    for buf, pad in ((c_hi, KPAD), (c_lo, KPAD), (t_hi, FPAD), (t_lo, FPAD), (s_hi, FPAD), (s_lo, FPAD)):
        edge = jnp.zeros((pad, 2 * G, LANES), BF16)
        buf[pl.ds(0, pad)] = edge
        buf[pl.ds(TILES + pad, pad)] = edge

    def along_z(t, carry):
        lanes = pl.ds(pl.multiple_of(t * LANES, LANES), LANES)
        for s in range(2):
            rows = pl.ds(s * G, G)
            high, low = split(cube[s, :, lanes])
            c_hi[t + KPAD, rows, :] = high
            c_lo[t + KPAD, rows, :] = low
            both = mm(z_in[...], jnp.concatenate([high, low, high], 0))
            kz[t, rows, :] = both[G:]
            high, low = split(both[:G])
            t_hi[t + FPAD, rows, :] = high
            t_lo[t + FPAD, rows, :] = low
        return carry

    lax.fori_loop(0, TILES, along_z, 0)
    group = 2

    def spread(hi, lo, table, count, first, acc):
        for d in range(count):
            high = hi[pl.ds(first + d, group)].reshape(group * 2 * G, LANES)
            low = lo[pl.ds(first + d, group)].reshape(group * 2 * G, LANES)
            term = mm(high, table[0, d]) + mm(low, table[0, d]) + mm(high, table[1, d])
            acc = term if acc is None else acc + term
        return acc

    def middle(i, carry):
        first = i * group
        grid = spread(t_hi, t_lo, into, 2 * FPAD + 1, first, None)
        for j in range(group):
            lanes = pl.ds(pl.multiple_of((first + j) * LANES, LANES), LANES)
            local = vfull[:, lanes]
            for s in range(2):
                low_row = (j * 2 + s) * G
                high, low = split(grid[low_row : low_row + G] * local)
                done = mm(z_out[...], jnp.concatenate([high, low, high], 0))
                high, low = split(done)
                s_hi[first + j + FPAD, pl.ds(s * G, G), :] = high
                s_lo[first + j + FPAD, pl.ds(s * G, G), :] = low
        return carry

    lax.fori_loop(0, TILES // group, middle, 0)

    def last(i, carry):
        first = i * group
        acc = kz[pl.ds(first, group)].reshape(group * 2 * G, LANES)
        acc = spread(c_hi, c_lo, kin, 2 * KPAD + 1, first, acc)
        acc = spread(s_hi, s_lo, back, 2 * FPAD + 1, first, acc)
        for j in range(group):
            lanes = pl.ds(pl.multiple_of((first + j) * LANES, LANES), LANES)
            for s in range(2):
                low_row = (j * 2 + s) * G
                out[s, :, lanes] = acc[low_row : low_row + G]
        return carry

    lax.fori_loop(0, TILES // group, last, 0)


def scatter_kernel(applied, pieces, own, send_sem, recv_sem):
    orb, box, _, _, _ = place()
    target = pl.ds(orb * SLOTS + 2 * box, 2)

    def source(to_orb, to_box):
        z_rows = pl.ds(pl.multiple_of(to_box * DEPTH + (to_orb // 32) * 8, 8), 8)
        return applied.at[:, z_rows, pl.ds(pl.multiple_of((to_orb % 32) * 128, 128), 128)]

    mine = pltpu.make_async_copy(source(orb, box), pieces.at[target], own)
    mine.start()

    def send(step, carry):
        to_orb = shifted(orb, step // BOX)
        to_box = (box + step % BOX) % BOX
        remote(source(to_orb, to_box), pieces.at[target], send_sem, recv_sem, to_orb, to_box).start()
        return carry

    lax.fori_loop(1, ORB * BOX, send, 0)
    mine.wait()
    rest = pieces.at[pl.ds(0, SLOTS * ORB - 2)]
    wait_for(rest, send_sem)
    wait_for(rest, recv_sem)


def reduce_kernel(
    psi_pieces, app_pieces, slots, mult, ext,
    part, rs, bb, resid, c_hi, c_lo, a_hi, a_lo, sems, own,
):
    orb, box, x, z, core = place()
    pieces2 = psi_pieces.reshape(SLOTS * ORB * 8, 128)
    applied2 = app_pieces.reshape(SLOTS * ORB * 8, 128)
    resid2 = resid.reshape(ORBS * 8, 128)
    pick = (
        lax.broadcasted_iota(jnp.int32, (ORBS, SLOTS * ORB), 1) == slots[...]
    ).astype(F32).astype(BF16)
    for k in range(8):
        lanes = pl.ds(k * 128, 128)
        for ref, hi, lo in ((pieces2, c_hi, c_lo), (applied2, a_hi, a_lo)):
            high, low = split(ref[pl.ds(k, SLOTS * ORB, stride=8), :])
            hi[:, lanes] = mm(pick, high).astype(BF16)
            lo[:, lanes] = mm(pick, low).astype(BF16)

    def dot_nt(left, right):
        return lax.dot_general(left, right, (((1,), (1,)), ((), ())), preferred_element_type=F32)

    scale = 1.0 / float(G**3)
    total = dot_nt(c_hi[...], a_hi[...]) + dot_nt(c_lo[...], a_hi[...]) + dot_nt(c_hi[...], a_lo[...])
    part[...] = (total * scale).reshape(16, 16, ORBS)

    a_me = x * 4 + box
    b_me = z * 2 + core

    def a_peer(step):
        return ((x + step // 4) % 4) * 16 + z * 2 + core, (box + step % 4) % 4

    def b_peer(step):
        return x * 16 + ((z + step // 2) % 8) * 2 + (core + step % 2) % 2, box

    def send_rows(step, carry):
        to_orb, to_box = a_peer(step)
        a_to = (to_orb // 16) * 4 + to_box
        remote(part.at[a_to], rs.at[a_me], sems.at[0], sems.at[1], to_orb, to_box).start()
        return carry

    lax.fori_loop(1, 16, send_rows, 0)
    rs[a_me] = part[a_me]
    wait_for(rs.at[pl.ds(0, 15)], sems.at[1])
    bb[b_me] = jnp.sum(rs[...], axis=0)

    def send_sum(step, carry):
        to_orb, to_box = b_peer(step)
        remote(bb.at[b_me], bb.at[b_me], sems.at[2], sems.at[3], to_orb, to_box).start()
        return carry

    lax.fori_loop(1, 16, send_sum, 0)
    wait_for(bb.at[pl.ds(0, 15)], sems.at[3])
    mult[a_me] = jnp.sum(bb[...], axis=0)

    def send_total(step, carry):
        to_orb, to_box = a_peer(step)
        remote(mult.at[a_me], mult.at[a_me], sems.at[4], sems.at[5], to_orb, to_box).start()
        return carry

    lax.fori_loop(1, 16, send_total, 0)
    wait_for(mult.at[pl.ds(0, 15)], sems.at[5])
    m_hi, m_lo = split(mult[...].reshape(ORBS, ORBS).T)
    for k in range(8):
        lanes = pl.ds(k * 128, 128)
        fix = mm(m_hi, c_hi[:, lanes]) + mm(m_hi, c_lo[:, lanes]) + mm(m_lo, c_hi[:, lanes])
        value = a_hi[:, lanes].astype(F32) + a_lo[:, lanes].astype(F32) - fix
        resid2[pl.ds(k, ORBS, stride=8), :] = value

    z_rows = pl.ds(pl.multiple_of(8 + (orb // 32) * 8, 8), 8)
    lanes = pl.ds(pl.multiple_of((orb % 32) * 128, 128), 128)
    landing = ext.at[:, z_rows, lanes]
    mine = pltpu.make_async_copy(resid.at[pl.ds(orb * OWN, OWN)], landing, own)
    mine.start()

    def send_resid(step, carry):
        to = shifted(orb, step)
        remote(resid.at[pl.ds(to * OWN, OWN)], landing, sems.at[6], sems.at[7], to, box).start()
        return carry

    lax.fori_loop(1, ORB, send_resid, 0)
    mine.wait()
    wait_for(resid.at[pl.ds(0, OWN * (ORB - 1))], sems.at[7])
    up = remote(ext.at[:, pl.ds(20, 4), :], ext.at[:, pl.ds(4, 4), :], sems.at[8], sems.at[9], orb, (box + 1) % BOX)
    down = remote(ext.at[:, pl.ds(8, 4), :], ext.at[:, pl.ds(24, 4), :], sems.at[10], sems.at[11], orb, (box + 3) % BOX)
    up.start()
    down.start()
    wait_for(part.at[pl.ds(0, 15)], sems.at[0])
    wait_for(bb.at[pl.ds(0, 15)], sems.at[2])
    wait_for(mult.at[pl.ds(0, 15)], sems.at[4])
    wait_for(resid.at[pl.ds(0, OWN * (ORB - 1))], sems.at[6])
    up.wait()
    down.wait()


def relax_kernel(ext, mult, resid_out, direct_out):
    orb = lax.axis_index("orb")
    box = lax.axis_index("box")
    lane = lax.broadcasted_iota(jnp.int32, (32, PLANE), 1)
    row = lax.broadcasted_iota(jnp.int32, (32, PLANE), 0)
    inside = ((row >= 8) | (box > 0)) & ((row < 24) | (box < BOX - 1))
    col = lane % G
    for n in range(OWN):
        which = orb * OWN + n
        line = mult[pl.ds(which, 1), :]
        keep = lax.broadcasted_iota(jnp.int32, (1, ORBS), 1) == which
        diagonal = jnp.sum(jnp.where(keep, line, 0.0), axis=1, keepdims=True)
        denominator = 2.0 * coupling_z + 4.0 * coupling_xy + 1.0 + jnp.abs(diagonal)
        inverse = 1.0 / denominator
        resid = jnp.where(inside, ext[n], 0.0)
        resid_out[n] = resid[8:24]
        now = resid * inverse
        for _ in range(SWEEPS):
            side = jnp.where(col != 0, pltpu.roll(now, 1, 1), 0.0)
            side = side + jnp.where(col != G - 1, pltpu.roll(now, PLANE - 1, 1), 0.0)
            side = side + jnp.where(lane >= G, pltpu.roll(now, G, 1), 0.0)
            side = side + jnp.where(lane < PLANE - G, pltpu.roll(now, PLANE - G, 1), 0.0)
            along_z = pltpu.roll(now, 1, 0) + pltpu.roll(now, 31, 0)
            now = jnp.where(inside, (resid + coupling_xy * side + coupling_z * along_z) * inverse, 0.0)
        direct_out[n] = now[8:24]


DMA = pltpu.SemaphoreType.DMA


def shape(*dims, dtype=F32):
    return jax.ShapeDtypeStruct(dims, dtype)


def local(psi, potential, orbital_slot):
    z_in, z_out, into, back, kin = [jnp.asarray(t) for t in tables()]
    params = pltpu.CompilerParams(has_side_effects=True, vmem_limit_bytes=VLIMIT)
    pieces, cube, vfull = pl.pallas_call(
        exchange_kernel,
        out_shape=[shape(SLOTS * ORB, 8, 128), shape(2, G, PLANE), shape(G, PLANE)],
        in_specs=[ANY] * 2,
        out_specs=[ANY] * 3,
        scratch_shapes=[DMA((3,))] + [DMA] * 6,
        compiler_params=params,
        name="exchange",
    )(psi, potential)
    bf = lambda pad: pltpu.VMEM((TILES + 2 * pad, 2 * G, LANES), BF16)
    applied = pl.pallas_call(
        apply_kernel,
        out_shape=shape(2, G, PLANE),
        in_specs=[VMEM] * 7,
        out_specs=VMEM,
        scratch_shapes=[bf(KPAD), bf(KPAD), bf(FPAD), bf(FPAD), bf(FPAD), bf(FPAD), pltpu.VMEM((TILES, 2 * G, LANES), F32)],
        compiler_params=pltpu.CompilerParams(vmem_limit_bytes=VLIMIT),
        name="filters",
    )(cube, vfull, z_in, z_out, into, back, kin)
    app_pieces = pl.pallas_call(
        scatter_kernel,
        out_shape=shape(SLOTS * ORB, 8, 128),
        in_specs=[ANY],
        out_specs=ANY,
        scratch_shapes=[DMA] * 3,
        compiler_params=params,
        name="scatter",
    )(applied)
    table = lambda: pltpu.VMEM((ORBS, 1024), BF16)
    mult, ext = pl.pallas_call(
        reduce_kernel,
        out_shape=[shape(16, 16, ORBS), shape(OWN, 32, PLANE)],
        in_specs=[VMEM] * 3,
        out_specs=[VMEM, VMEM],
        scratch_shapes=[
            pltpu.VMEM((16, 16, ORBS), F32),
            pltpu.VMEM((16, 16, ORBS), F32),
            pltpu.VMEM((16, 16, ORBS), F32),
            pltpu.VMEM((ORBS, 8, 128), F32),
            table(), table(), table(), table(),
            DMA((12,)),
            DMA,
        ],
        compiler_params=params,
        name="reduce",
    )(pieces, app_pieces, orbital_slot.reshape(ORBS, 1))
    mult = mult.reshape(ORBS, ORBS)
    residual, direction = pl.pallas_call(
        relax_kernel,
        out_shape=[shape(OWN, DEPTH, PLANE)] * 2,
        in_specs=[VMEM] * 2,
        out_specs=[VMEM] * 2,
        compiler_params=pltpu.CompilerParams(vmem_limit_bytes=VLIMIT),
        name="relax",
    )(ext, mult)
    return residual, direction, mult


def solution(mesh):
    in_specs = (P("orb", "box", None), P("box", None), P())
    out_specs = (P("orb", "box", None), P("orb", "box", None), P())
    return jax.shard_map(local, mesh=mesh, in_specs=in_specs, out_specs=out_specs, check_vma=False)
```

time: 619 us -> 245 us (0.40); the launches traced: 610 us -> 245 us
  waiting for transfers between devices: 352 us -> 0 us
  Pallas kernels: 0 us -> 243 us
  local copies, waits for them, and re-layouts: 72.4 us -> 1.51 us
  blocking collectives: 68 us -> 0 us
  matrix products: 52 us -> 0 us
  starting transfers between devices: 43.1 us -> 0 us
  between operations: 14.6 us -> 0.67 us
  other arithmetic: 7.64 us -> 0 us
    psum x1 -> x0, waiting for transfers between devices: 248 us -> none  [local(): multipliers = lax.psum(partial_value, ('orb', 'box'))]
    pallas_call x0 -> x5, Pallas kernels: none -> 243 us  [the longest x1 73.8 us: local(): pl.pallas_call(reduce_kernel, out_shape=[shape(16, 16, ORBS), shape(OWN,...]
    all_to_all x2 -> x0, waiting for transfers between devices: 74 us -> none  [the longest x1 49.3 us: local(): lax.all_to_all(flattened, 'orb', split_axis=1, concat_axis=0, tiled=True)]
    all_to_all x2 -> x0, blocking collectives: 68 us -> none  [the longest x1 34.5 us: local(): lax.all_to_all(coeff_rows, 'orb', split_axis=0, concat_axis=1, tiled=True)]
    dot_general x11 -> x0, matrix products: 52 us -> none  [the longest x3 22.9 us: along_rows(): jnp.einsum('nzyx,yq->nzqx', split_rows, jnp.asarray(matrix, dtype=jnp.flo...]
    ppermute x10 -> x0, waiting for transfers between devices: 30.4 us -> none  [the longest x5 23.1 us: extended_2(): lax.ppermute(lax.slice_in_dim(block, 0, width, axis=dim), axis, backward)]
    reshape x10 -> x1, local copies, waits for them, and re-layouts: 26.2 us -> 0.8 us  [local(): orbital_slot.reshape(ORBS, 1)]
    ppermute x10 -> x0, starting transfers between devices: 22.3 us -> none  [the longest x5 15.8 us: extended_2(): lax.ppermute(lax.slice_in_dim(block, block.shape[dim] - width, None, axis...]
  transfers between devices with their start and end apart: 13 -> 0, of which waited for: 13 -> 0; matrix products, arithmetic and copies ran while one was open for 4% -> 0% of each run, Pallas kernels for 0% -> 0%
where the time goes in v1:
time: 245 us
  Pallas kernels  243 us (99%)
    pallas_call x1, Pallas kernels, local(): pl.pallas_call(reduce_kernel, out_shape=[shape(16, 16, ORBS), shape(OWN,...  73.8 us
    pallas_call x1, Pallas kernels, local(): pl.pallas_call(exchange_kernel, out_shape=[shape(SLOTS * ORB, 8, 128), sh...  66.6 us
    pallas_call x1, Pallas kernels, local(): pl.pallas_call(scatter_kernel, out_shape=shape(SLOTS * ORB, 8, 128), in_s...  63.4 us
    pallas_call x1, Pallas kernels, local(): pl.pallas_call(apply_kernel, out_shape=shape(2, G, PLANE), in_specs=[VMEM...  28.2 us
    pallas_call x1, Pallas kernels, local(): pl.pallas_call(relax_kernel, out_shape=[shape(OWN, DEPTH, PLANE)] * 2, in...  10.6 us

profile of v1, /device:TPU:2, one launch (start us, length us, event | category | flops | bytes accessed | tf_op | source)
XLA Modules:
  0.0 244.8 jit_solution(16934153315739899951)
XLA Ops:
  0.6 66.6 %exchange.1 = (f32[512,8,128]{2,1,0:T(8,128)}, f32[2,64,4096]{2,1,0:T(8,128)}, f32[64,4096]{1,0:T(8,128)}) custom-call(f32[8,16,4096]{2,1,0:T(8,128)} %psi.1, f32[16,4096]{1,0:T(8,128)} %pot.1), custom_call_target="tpu_custom_call" | custom-call | tf_op jit(solution)/shard_map/exchange/pallas_call | solution.py:403
  67.2 28.2 %filters.1.applied = f32[2,64,4096]{2,1,0:T(8,128)} custom-call(f32[2,64,4096]{2,1,0:T(8,128)} %get-tuple-element.11.cube, f32[64,4096]{1,0:T(8,128)} %get-tuple-element.12.vfull, bf16[128,192]{1,0:T(8,128)(2,1)} %constant.10.clone.z_in, bf16[64,192]{1,0:T(8,128)(2,1)} %constant.11.clone.z_out, bf16[2,5,256,256]{3,2,1,0:T(8,128)(2,1)} %constant.12.clone.into, ...), custom_call_target="tpu_custom_call" | custom-call | tf_op jit(solution)/shard_map/filters/pallas_call | solution.py:413
  95.4 0.0 copy-start.1
  95.4 63.4 %scatter.1.app_pieces = f32[512,8,128]{2,1,0:T(8,128)} custom-call(f32[2,64,4096]{2,1,0:T(8,128)} %filters.1.applied), custom_call_target="tpu_custom_call" | custom-call | tf_op jit(solution)/shard_map/scatter/pallas_call | solution.py:422
  158.8 0.0 copy-done.1
  158.9 0.8 copy.11.slots
  159.7 73.8 %reduce.1 = (f32[16,16,256]{2,1,0:T(8,128)}, f32[4,32,4096]{2,1,0:T(8,128)}) custom-call(f32[512,8,128]{2,1,0:T(8,128)} %get-tuple-element.10.psi_pieces, f32[512,8,128]{2,1,0:T(8,128)} %scatter.1.app_pieces, s32[256,1]{1,0:T(8,128)} %copy.11.slots), custom_call_target="tpu_custom_call" | custom-call | tf_op jit(solution)/shard_map/reduce/pallas_call | solution.py:432
  233.5 0.0 copy-start
  233.5 10.6 %relax.1 = (f32[4,16,4096]{2,1,0:T(8,128)}, f32[4,16,4096]{2,1,0:T(8,128)}) custom-call(f32[4,32,4096]{2,1,0:T(8,128)} %get-tuple-element.13.ext, f32[256,256]{1,0:T(8,128)} %bitcast.2), custom_call_target="tpu_custom_call" | custom-call | tf_op jit(solution)/shard_map/relax/pallas_call | solution.py:450
  244.1 0.0 copy-done
  244.1 0.7 copy.13
Async XLA Ops:
  95.4 63.4 %copy-start.1 = (s32[256]{0:T(256)S(1)}, s32[256]{0:T(256)}, u32[]{:S(2)}) copy-start(s32[256]{0:T(256)} %param.10) | copy-start | bytes 3076
  233.5 10.6 %copy-start = (f32[16,16,256]{2,1,0:T(8,128)S(1)}, f32[16,16,256]{2,1,0:T(8,128)}, u32[]{:S(2)}) copy-start(f32[16,16,256]{2,1,0:T(8,128)} %get-tuple-element.14) | copy-start | bytes 786436

commit v2 on v1

v2 whole, which is shorter than its diff:
```python
import math

import jax
import jax.numpy as jnp
import ml_dtypes
import numpy as np
from jax import lax
from jax.experimental import pallas as pl
from jax.experimental.pallas import tpu as pltpu
from jax.sharding import PartitionSpec as P

G = 64
MTAPS = 16
KREACH = 14
SWEEPS = 4
ORB, BOX = 64, 4
SLOTS, ORBS, OWN = 8, 256, 4
DEPTH = 16
PLANE = G * G
LANES = 256
TILES = PLANE // LANES
FPAD, KPAD = 2, 4

coupling_z = 4.0
coupling_xy = 1.0

F32, BF16 = jnp.float32, jnp.bfloat16
ANY = pl.BlockSpec(memory_space=pl.ANY)
VMEM = pl.BlockSpec(memory_space=pltpu.VMEM)
VLIMIT = 56 * 2**20


def magic_weights(tap_count):
    half_len = tap_count // 2
    offsets = np.arange(1 - half_len, half_len + 1) * 1.0
    weights = np.ones(tap_count)
    for index_a in range(tap_count):
        for index_b in range(tap_count):
            if index_b != index_a:
                weights[index_a] *= (0.25 - offsets[index_b]) / (
                    offsets[index_a] - offsets[index_b]
                )
    return weights


def second_weights(reach_cells):
    factor = math.factorial(reach_cells) ** 2
    weights = np.zeros(2 * reach_cells + 1)
    for distance in range(1, reach_cells + 1):
        entry_value = (
            2.0
            * (-1) ** (distance + 1)
            * factor
            / (
                distance
                * distance
                * math.factorial(reach_cells - distance)
                * math.factorial(reach_cells + distance)
            )
        )
        weights[reach_cells + distance] = entry_value
        weights[reach_cells - distance] = entry_value
    weights[reach_cells] = -weights.sum()
    return -0.5 * weights


def banded(row_count, col_count, row_start, col_start, weights, offset_low):
    row_index = np.arange(row_count)[:, None] + row_start
    col_index = np.arange(col_count)[None, :] + col_start
    position = row_index - col_index - offset_low
    inside = (position >= 0) & (position < len(weights))
    return np.where(inside, weights[np.clip(position, 0, len(weights) - 1)], 0.0)


def halves(table):
    table = np.asarray(table, np.float32)
    high = table.astype(ml_dtypes.bfloat16)
    low = (table - high.astype(np.float32)).astype(ml_dtypes.bfloat16)
    return high, low


def tables():
    magic = magic_weights(MTAPS)
    kinetic_row = second_weights(KREACH)
    forward = banded(G, G, 0, 0, magic, 1 - MTAPS // 2)
    kinetic = banded(G, G, 0, 0, kinetic_row, -KREACH)
    rows = LANES // G

    def beside(high, low):
        return np.concatenate([high, high, low], 1)

    z_in = beside(*halves(np.concatenate([forward.T, kinetic], 0)))
    z_out = beside(*halves(forward))
    into, back, kin = [], [], []
    for step in range(-FPAD, FPAD + 1):
        block = banded(rows, rows, rows * step, 0, magic, 1 - MTAPS // 2)
        into.append(np.kron(block, forward))
        block = banded(rows, rows, -rows * step, 0, magic, 1 - MTAPS // 2).T
        back.append(np.kron(block, forward.T))
    for step in range(-KPAD, KPAD + 1):
        block = np.kron(banded(rows, rows, rows * step, 0, kinetic_row, -KREACH), np.eye(G))
        if step == 0:
            block = block + np.kron(np.eye(rows), kinetic)
        kin.append(block)
    return [z_in, z_out] + [np.stack(halves(np.stack(m))) for m in (into, back, kin)]


def split(values):
    high = values.astype(BF16)
    return high, (values - high.astype(F32)).astype(BF16)


def mm(left, right):
    return jnp.dot(left, right, preferred_element_type=F32)


def place():
    orb = lax.axis_index("orb")
    box = lax.axis_index("box")
    return orb, box, orb // 16, (orb // 2) % 8, orb % 2


def shifted(orb, step):
    x, z, core = orb // 16, (orb // 2) % 8, orb % 2
    dx, dz, dc = step // 16, (step // 2) % 8, step % 2
    return ((x + dx) % 4) * 16 + ((z + dz) % 8) * 2 + (core + dc) % 2


def remote(src, dst, send, recv, orb, box):
    return pltpu.make_async_remote_copy(
        src_ref=src,
        dst_ref=dst,
        send_sem=send,
        recv_sem=recv,
        device_id={"orb": orb, "box": box},
        device_id_type=pl.DeviceIdType.MESH,
    )


def wait_for(ref, sem):
    pltpu.make_async_copy(ref, ref, sem).wait()


def tile_of(orb):
    return pl.ds(pl.multiple_of((orb // 32) * 8, 8), 8), pl.ds(
        pl.multiple_of((orb % 32) * 128, 128), 128
    )


CHUNKS = 4


def greet(orb, box, x, z, core, plane_sem):
    barrier = pltpu.get_barrier_semaphore()

    def signal(sem, to_orb, to_box):
        pl.semaphore_signal(
            sem, inc=1, device_id={"orb": to_orb, "box": to_box}, device_id_type=pl.DeviceIdType.MESH
        )

    def along_z(step, carry):
        signal(barrier, x * 16 + ((z + step) % 8) * 2 + core, box)
        return carry

    def across(sem):
        def body(step, carry):
            signal(sem, ((x + step // 2) % 4) * 16 + z * 2 + (core + step % 2) % 2, box)
            return carry

        return body

    def beside(sem):
        for step in range(1, BOX):
            signal(sem, orb, (box + step) % BOX)

    beside(barrier)
    lax.fori_loop(1, 8, along_z, 0)
    lax.fori_loop(1, 8, across(barrier), 0)
    pl.semaphore_wait(barrier, 7 + 7 + 3)
    lax.fori_loop(1, 8, across(plane_sem), 0)
    return beside


def filters(cube, vfull, z_in, z_out, into, back, kin, out, c_hi, c_lo, t_hi, t_lo, s_hi, s_lo, kz, arrived, tabled):
    for buf, pad in ((c_hi, KPAD), (c_lo, KPAD), (t_hi, FPAD), (t_lo, FPAD), (s_hi, FPAD), (s_lo, FPAD)):
        edge = jnp.zeros((pad, 2 * G, LANES), BF16)
        buf[pl.ds(0, pad)] = edge
        buf[pl.ds(TILES + pad, pad)] = edge

    def along_z(t, carry):
        lanes = pl.ds(pl.multiple_of(t * LANES, LANES), LANES)
        for s in range(2):
            rows = pl.ds(s * G, G)
            high, low = split(cube[s, :, lanes])
            c_hi[t + KPAD, rows, :] = high
            c_lo[t + KPAD, rows, :] = low
            both = mm(z_in[...], jnp.concatenate([high, low, high], 0))
            kz[t, rows, :] = both[G:]
            high, low = split(both[:G])
            t_hi[t + FPAD, rows, :] = high
            t_lo[t + FPAD, rows, :] = low
        return carry

    tabled()
    per = TILES // CHUNKS
    for chunk in range(CHUNKS):
        arrived(chunk)
        lax.fori_loop(chunk * per, (chunk + 1) * per, along_z, 0)
    group = 2

    def spread(hi, lo, table, count, first, acc):
        for d in range(count):
            high = hi[pl.ds(first + d, group)].reshape(group * 2 * G, LANES)
            low = lo[pl.ds(first + d, group)].reshape(group * 2 * G, LANES)
            term = mm(high, table[0, d]) + mm(low, table[0, d]) + mm(high, table[1, d])
            acc = term if acc is None else acc + term
        return acc

    def middle(i, carry):
        first = i * group
        grid = spread(t_hi, t_lo, into, 2 * FPAD + 1, first, None)
        for j in range(group):
            lanes = pl.ds(pl.multiple_of((first + j) * LANES, LANES), LANES)
            local = vfull[:, lanes]
            for s in range(2):
                low_row = (j * 2 + s) * G
                high, low = split(grid[low_row : low_row + G] * local)
                done = mm(z_out[...], jnp.concatenate([high, low, high], 0))
                high, low = split(done)
                s_hi[first + j + FPAD, pl.ds(s * G, G), :] = high
                s_lo[first + j + FPAD, pl.ds(s * G, G), :] = low
        return carry

    lax.fori_loop(0, TILES // group, middle, 0)

    def last(i, carry):
        first = i * group
        acc = kz[pl.ds(first, group)].reshape(group * 2 * G, LANES)
        acc = spread(c_hi, c_lo, kin, 2 * KPAD + 1, first, acc)
        acc = spread(s_hi, s_lo, back, 2 * FPAD + 1, first, acc)
        for j in range(group):
            lanes = pl.ds(pl.multiple_of((first + j) * LANES, LANES), LANES)
            for s in range(2):
                low_row = (j * 2 + s) * G
                out[s, :, lanes] = acc[low_row : low_row + G]
        return carry

    lax.fori_loop(0, TILES // group, last, 0)


def dot_nt(left, right):
    return lax.dot_general(left, right, (((1,), (1,)), ((), ())), preferred_element_type=F32)


def relax(resid, mult, which, box, resid_out, direct_out):
    lane = lax.broadcasted_iota(jnp.int32, (32, PLANE), 1)
    row = lax.broadcasted_iota(jnp.int32, (32, PLANE), 0)
    inside = ((row >= 8) | (box > 0)) & ((row < 24) | (box < BOX - 1))
    col = lane % G
    line = mult[which // 16, pl.ds(which % 16, 1), :]
    keep = lax.broadcasted_iota(jnp.int32, (1, ORBS), 1) == which
    diagonal = jnp.sum(jnp.where(keep, line, 0.0), axis=1, keepdims=True)
    denominator = 2.0 * coupling_z + 4.0 * coupling_xy + 1.0 + jnp.abs(diagonal)
    inverse = 1.0 / denominator
    resid = jnp.where(inside, resid, 0.0)
    resid_out[...] = resid[8:24]
    now = resid * inverse
    for _ in range(SWEEPS):
        side = jnp.where(col != 0, pltpu.roll(now, 1, 1), 0.0)
        side = side + jnp.where(col != G - 1, pltpu.roll(now, PLANE - 1, 1), 0.0)
        side = side + jnp.where(lane >= G, pltpu.roll(now, G, 1), 0.0)
        side = side + jnp.where(lane < PLANE - G, pltpu.roll(now, PLANE - G, 1), 0.0)
        along_z = pltpu.roll(now, 1, 0) + pltpu.roll(now, 31, 0)
        now = jnp.where(inside, (resid + coupling_xy * side + coupling_z * along_z) * inverse, 0.0)
    direct_out[...] = now[8:24]


def step_kernel(
    psi, pot, slots, z_in_h, z_out_h, into_h, back_h, kin_h,
    resid_out, direct_out, mult,
    pieces, app_pieces, cube, vfull, applied,
    z_in, z_out, into, back, kin,
    f_c_hi, f_c_lo, f_t_hi, f_t_lo, f_s_hi, f_s_lo, kz,
    part, rs, bb, resid, c_hi, c_lo, a_hi, a_lo, ext,
    own, y_send, y_recv, v_sem, p_sem, a_sem, r_sem, f_send, f_recv, h_send, h_recv, tab, plane_sem, all_sem,
):
    orb, box, x, z, core = place()
    table_copies = [
        pltpu.make_async_copy(src, dst, tab.at[i])
        for i, (src, dst) in enumerate(
            ((z_in_h, z_in), (z_out_h, z_out), (into_h, into), (back_h, back), (kin_h, kin))
        )
    ]
    for copy in table_copies:
        copy.start()
    slab = pl.ds(pl.multiple_of(box * DEPTH, DEPTH), DEPTH)
    width = PLANE // CHUNKS
    v_mine = pltpu.make_async_copy(pot, vfull.at[slab, :], own.at[0])
    v_mine.start()
    target = pl.ds(pl.multiple_of(orb * SLOTS, SLOTS), SLOTS)
    z_rows, lanes = tile_of(orb)
    p_mine = pltpu.make_async_copy(psi.at[:, z_rows, lanes], pieces.at[target], own.at[1])
    p_mine.start()
    c_mine = pltpu.make_async_copy(psi.at[pl.ds(2 * box, 2)], cube.at[:, slab, :], own.at[2])
    c_mine.start()

    beside = greet(orb, box, x, z, core, plane_sem)
    for chunk in range(CHUNKS):
        cols = pl.ds(chunk * width, width)
        for step in range(1, BOX):
            to = (box + step) % BOX
            remote(
                psi.at[pl.ds(2 * to, 2), :, cols], cube.at[:, slab, cols],
                y_send.at[chunk], y_recv.at[chunk], orb, to,
            ).start()
    for step in range(1, BOX):
        remote(pot, vfull.at[slab, :], v_sem.at[0], v_sem.at[1], orb, (box + step) % BOX).start()
    pl.semaphore_wait(plane_sem, 7)

    def send_psi(step, carry):
        to = shifted(orb, step)
        z_rows, lanes = tile_of(to)
        remote(psi.at[:, z_rows, lanes], pieces.at[target], p_sem.at[0], p_sem.at[1], to, box).start()
        return carry

    lax.fori_loop(1, ORB, send_psi, 0)
    beside(all_sem)

    def tabled():
        for copy in table_copies:
            copy.wait()

    def arrived(chunk):
        if chunk == 0:
            c_mine.wait()
        third = cube.at[:, pl.ds(0, 3 * DEPTH), pl.ds(chunk * width, width)]
        wait_for(third, y_recv.at[chunk])
        if chunk == CHUNKS - 1:
            v_mine.wait()
            wait_for(vfull.at[pl.ds(0, 3 * DEPTH)], v_sem.at[1])

    filters(
        cube, vfull, z_in, z_out, into, back, kin, applied,
        f_c_hi, f_c_lo, f_t_hi, f_t_lo, f_s_hi, f_s_lo, kz, arrived, tabled,
    )
    pl.semaphore_wait(all_sem, BOX - 1)

    a_target = pl.ds(orb * SLOTS + 2 * box, 2)

    def source(to_orb, to_box):
        z_rows = pl.ds(pl.multiple_of(to_box * DEPTH + (to_orb // 32) * 8, 8), 8)
        return applied.at[:, z_rows, pl.ds(pl.multiple_of((to_orb % 32) * 128, 128), 128)]

    a_mine = pltpu.make_async_copy(source(orb, box), app_pieces.at[a_target], own.at[3])
    a_mine.start()

    def send_applied(step, carry):
        to_orb = shifted(orb, step // BOX)
        to_box = (box + step % BOX) % BOX
        remote(
            source(to_orb, to_box), app_pieces.at[a_target], a_sem.at[0], a_sem.at[1], to_orb, to_box
        ).start()
        return carry

    lax.fori_loop(1, ORB * BOX, send_applied, 0)

    pieces2 = pieces.reshape(SLOTS * ORB * 8, 128)
    applied2 = app_pieces.reshape(SLOTS * ORB * 8, 128)
    resid2 = resid.reshape(ORBS * 8, 128)
    pick = (
        lax.broadcasted_iota(jnp.int32, (ORBS, SLOTS * ORB), 1) == slots[...]
    ).astype(F32).astype(BF16)

    def choose(ref, hi, lo):
        for k in range(8):
            lanes = pl.ds(k * 128, 128)
            high, low = split(ref[pl.ds(k, SLOTS * ORB, stride=8), :])
            hi[:, lanes] = mm(pick, high).astype(BF16)
            lo[:, lanes] = mm(pick, low).astype(BF16)

    p_mine.wait()
    wait_for(pieces.at[pl.ds(0, SLOTS * (ORB - 1))], p_sem.at[1])
    choose(pieces2, c_hi, c_lo)
    a_mine.wait()
    wait_for(app_pieces.at[pl.ds(0, SLOTS * ORB - 2)], a_sem.at[1])
    choose(applied2, a_hi, a_lo)

    scale = 1.0 / float(G**3)
    total = dot_nt(c_hi[...], a_hi[...]) + dot_nt(c_lo[...], a_hi[...]) + dot_nt(c_hi[...], a_lo[...])
    part[...] = (total * scale).reshape(16, 16, ORBS)

    a_me = x * 4 + box
    b_me = z * 2 + core

    def a_peer(step):
        return ((x + step // 4) % 4) * 16 + z * 2 + core, (box + step % 4) % 4

    def b_peer(step):
        return x * 16 + ((z + step // 2) % 8) * 2 + (core + step % 2) % 2, box

    def send_rows(step, carry):
        to_orb, to_box = a_peer(step)
        a_to = (to_orb // 16) * 4 + to_box
        remote(part.at[a_to], rs.at[a_me], r_sem.at[0], r_sem.at[1], to_orb, to_box).start()
        return carry

    lax.fori_loop(1, 16, send_rows, 0)
    rs[a_me] = part[a_me]
    wait_for(rs.at[pl.ds(0, 15)], r_sem.at[1])
    bb[b_me] = jnp.sum(rs[...], axis=0)

    def send_sum(step, carry):
        to_orb, to_box = b_peer(step)
        remote(bb.at[b_me], bb.at[b_me], r_sem.at[2], r_sem.at[3], to_orb, to_box).start()
        return carry

    lax.fori_loop(1, 16, send_sum, 0)
    wait_for(bb.at[pl.ds(0, 15)], r_sem.at[3])
    mult[a_me] = jnp.sum(bb[...], axis=0)

    def send_total(step, carry):
        to_orb, to_box = a_peer(step)
        remote(mult.at[a_me], mult.at[a_me], r_sem.at[4], r_sem.at[5], to_orb, to_box).start()
        return carry

    lax.fori_loop(1, 16, send_total, 0)
    wait_for(mult.at[pl.ds(0, 15)], r_sem.at[5])
    m_hi, m_lo = split(mult[...].reshape(ORBS, ORBS).T)
    for k in range(8):
        lanes = pl.ds(k * 128, 128)
        fix = mm(m_hi, c_hi[:, lanes]) + mm(m_hi, c_lo[:, lanes]) + mm(m_lo, c_hi[:, lanes])
        value = a_hi[:, lanes].astype(F32) + a_lo[:, lanes].astype(F32) - fix
        resid2[pl.ds(k, ORBS, stride=8), :] = value

    z_rows = pl.ds(pl.multiple_of(8 + (orb // 32) * 8, 8), 8)
    lanes = pl.ds(pl.multiple_of((orb % 32) * 128, 128), 128)
    r_mine = []
    for n in range(OWN):
        landing = ext.at[pl.ds(n, 1), z_rows, lanes]
        copy = pltpu.make_async_copy(resid.at[pl.ds(orb * OWN + n, 1)], landing, own.at[4 + n])
        copy.start()
        r_mine.append(copy)

        def send_resid(step, carry, n=n, landing=landing):
            to = shifted(orb, step)
            remote(resid.at[pl.ds(to * OWN + n, 1)], landing, f_send, f_recv.at[n], to, box).start()
            return carry

        lax.fori_loop(1, ORB, send_resid, 0)

    def halo(n):
        one = pl.ds(n, 1)
        up = remote(
            ext.at[one, pl.ds(20, 4), :], ext.at[one, pl.ds(4, 4), :],
            h_send.at[2 * n], h_recv.at[2 * n], orb, (box + 1) % BOX,
        )
        down = remote(
            ext.at[one, pl.ds(8, 4), :], ext.at[one, pl.ds(24, 4), :],
            h_send.at[2 * n + 1], h_recv.at[2 * n + 1], orb, (box + 3) % BOX,
        )
        up.start()
        down.start()
        return up, down

    def finish(n, pair):
        for copy in pair:
            copy.wait()
        relax(ext[n], mult, orb * OWN + n, box, resid_out.at[n], direct_out.at[n])

    pair = None
    for n in range(OWN):
        r_mine[n].wait()
        wait_for(resid.at[pl.ds(0, ORB - 1)], f_recv.at[n])
        following = halo(n)
        if pair is not None:
            finish(n - 1, pair)
        pair = following
    for chunk in range(CHUNKS):
        wait_for(cube.at[:, pl.ds(0, 3 * DEPTH), pl.ds(chunk * width, width)], y_send.at[chunk])
    wait_for(vfull.at[pl.ds(0, 3 * DEPTH)], v_sem.at[0])
    wait_for(pieces.at[pl.ds(0, SLOTS * (ORB - 1))], p_sem.at[0])
    wait_for(app_pieces.at[pl.ds(0, SLOTS * ORB - 2)], a_sem.at[0])
    wait_for(part.at[pl.ds(0, 15)], r_sem.at[0])
    wait_for(bb.at[pl.ds(0, 15)], r_sem.at[2])
    wait_for(mult.at[pl.ds(0, 15)], r_sem.at[4])
    wait_for(resid.at[pl.ds(0, OWN * (ORB - 1))], f_send)
    finish(OWN - 1, pair)


DMA = pltpu.SemaphoreType.DMA
REGULAR = pltpu.SemaphoreType.REGULAR


def shape(*dims, dtype=F32):
    return jax.ShapeDtypeStruct(dims, dtype)


def local(psi, potential, orbital_slot):
    consts = [jnp.asarray(t) for t in tables()]
    v32 = lambda *dims: pltpu.VMEM(dims, F32)
    v16 = lambda *dims: pltpu.VMEM(dims, BF16)
    padded = lambda pad: v16(TILES + 2 * pad, 2 * G, LANES)
    residual, direction, mult = pl.pallas_call(
        step_kernel,
        out_shape=[shape(OWN, DEPTH, PLANE), shape(OWN, DEPTH, PLANE), shape(16, 16, ORBS)],
        in_specs=[ANY, ANY, VMEM] + [ANY] * 5,
        out_specs=[VMEM] * 3,
        scratch_shapes=[
            v32(SLOTS * ORB, 8, 128), v32(SLOTS * ORB, 8, 128),
            v32(2, G, PLANE), v32(G, PLANE), v32(2, G, PLANE),
        ]
        + [v16(*t.shape) for t in consts]
        + [padded(KPAD)] * 2 + [padded(FPAD)] * 4 + [v32(TILES, 2 * G, LANES)]
        + [v32(16, 16, ORBS)] * 3 + [v32(ORBS, 8, 128)]
        + [v16(ORBS, 1024)] * 4 + [v32(OWN, 32, PLANE)]
        + [
            DMA((8,)), DMA((CHUNKS,)), DMA((CHUNKS,)), DMA((2,)), DMA((2,)), DMA((2,)), DMA((6,)),
            DMA, DMA((OWN,)), DMA((2 * OWN,)), DMA((2 * OWN,)), DMA((5,)), REGULAR, REGULAR,
        ],
        compiler_params=pltpu.CompilerParams(
            has_side_effects=True, vmem_limit_bytes=VLIMIT, collective_id=0
        ),
        name="orbital_step",
    )(psi, potential, orbital_slot.reshape(ORBS, 1), *consts)
    return residual, direction, mult.reshape(ORBS, ORBS)


def solution(mesh):
    in_specs = (P("orb", "box", None), P("box", None), P())
    out_specs = (P("orb", "box", None), P("orb", "box", None), P())
    return jax.shard_map(local, mesh=mesh, in_specs=in_specs, out_specs=out_specs, check_vma=False)
```

time: 245 us -> 183 us (0.75)
  Pallas kernels: 243 us -> 176 us
  local copies, waits for them, and re-layouts: 1.51 us -> 5.53 us
    pallas_call x5 -> x1, Pallas kernels: 243 us -> 176 us  [local(): pl.pallas_call(step_kernel, out_shape=[shape(OWN, DEPTH, PLANE), shape(OW...]
    unnamed x5 -> x7, local copies, waits for them, and re-layouts: 0.71 us -> 4.05 us
where the time goes in v2:
time: 183 us; the launch traced here: 182 us
  Pallas kernels  176 us (96%)
  local copies, waits for them, and re-layouts  5.53 us (3%)
    pallas_call x1, Pallas kernels, local(): pl.pallas_call(step_kernel, out_shape=[shape(OWN, DEPTH, PLANE), shape(OW...  176 us
    unnamed x7, local copies, waits for them, and re-layouts  4.05 us

profile of v2, /device:TPU:2, one launch (start us, length us, event | category | flops | bytes accessed | tf_op | source)
XLA Modules:
  0.0 181.8 jit_solution(1669704872724586054)
XLA Ops:
  0.6 1.5 copy.11.slots
  2.1 175.7 %orbital_step.1 = (f32[4,16,4096]{2,1,0:T(8,128)}, f32[4,16,4096]{2,1,0:T(8,128)}, f32[16,16,256]{2,1,0:T(8,128)}) custom-call(f32[8,16,4096]{2,1,0:T(8,128)} %psi.1, f32[16,4096]{1,0:T(8,128)} %pot.1, s32[256,1]{1,0:T(8,128)} %copy.11.slots, bf16[128,192]{1,0:T(8,128)(2,1)} %constant.10.clone.z_in_h, bf16[64,192]{1,0:T(8,128)(2,1)} %constant.11.clone.z_out_h, ...), custom_call_target="tpu_custom_call" | custom-call | tf_op jit(solution)/shard_map/orbital_step/pallas_call | solution.py:503
  177.8 0.0 copy-start
  177.8 0.0 copy-start.1
  177.8 2.4 %copy.15 = f32[4,16,4096]{2,1,0:T(8,128)} copy(f32[4,16,4096]{2,1,0:T(8,128)} %get-tuple-element.12) | data formatting | bytes 2097152
  180.2 0.0 copy-done
  180.2 1.0 copy.16
  181.1 0.0 copy-done.1
  181.1 0.7 copy.17
Async XLA Ops:
  177.8 2.4 %copy-start = (f32[4,16,4096]{2,1,0:T(8,128)S(1)}, f32[4,16,4096]{2,1,0:T(8,128)}, u32[]{:S(2)}) copy-start(f32[4,16,4096]{2,1,0:T(8,128)} %get-tuple-element.13) | copy-start | bytes 3145732
  177.8 3.4 %copy-start.1 = (f32[16,16,256]{2,1,0:T(8,128)S(1)}, f32[16,16,256]{2,1,0:T(8,128)}, u32[]{:S(2)}) copy-start(f32[16,16,256]{2,1,0:T(8,128)} %get-tuple-element.8) | copy-start | bytes 786436

commit v3 on v2

--- a/solution.py
+++ b/solution.py
@@ -201,11 +201,6 @@
             t_lo[t + FPAD, rows, :] = low
         return carry
 
-    tabled()
-    per = TILES // CHUNKS
-    for chunk in range(CHUNKS):
-        arrived(chunk)
-        lax.fori_loop(chunk * per, (chunk + 1) * per, along_z, 0)
     group = 2
 
     def spread(hi, lo, table, count, first, acc):
@@ -231,12 +226,29 @@
                 s_lo[first + j + FPAD, pl.ds(s * G, G), :] = low
         return carry
 
-    lax.fori_loop(0, TILES // group, middle, 0)
+    def kinetic(i, carry):
+        first = i * group
+        acc = kz[pl.ds(first, group)].reshape(group * 2 * G, LANES)
+        acc = spread(c_hi, c_lo, kin, 2 * KPAD + 1, first, acc)
+        kz[pl.ds(first, group)] = acc.reshape(group, 2 * G, LANES)
+        return carry
+
+    tabled()
+    per = TILES // CHUNKS
+    for chunk in range(CHUNKS - 1):
+        arrived(chunk)
+        lax.fori_loop(chunk * per, (chunk + 1) * per, along_z, 0)
+    early = (TILES - per - KPAD) // group
+    lax.fori_loop(0, early, kinetic, 0)
+    lax.fori_loop(0, early, middle, 0)
+    arrived(CHUNKS - 1)
+    lax.fori_loop(TILES - per, TILES, along_z, 0)
+    lax.fori_loop(early, TILES // group, middle, 0)
+    lax.fori_loop(early, TILES // group, kinetic, 0)
 
     def last(i, carry):
         first = i * group
         acc = kz[pl.ds(first, group)].reshape(group * 2 * G, LANES)
-        acc = spread(c_hi, c_lo, kin, 2 * KPAD + 1, first, acc)
         acc = spread(s_hi, s_lo, back, 2 * FPAD + 1, first, acc)
         for j in range(group):
             lanes = pl.ds(pl.multiple_of((first + j) * LANES, LANES), LANES)
@@ -257,7 +269,7 @@
     row = lax.broadcasted_iota(jnp.int32, (32, PLANE), 0)
     inside = ((row >= 8) | (box > 0)) & ((row < 24) | (box < BOX - 1))
     col = lane % G
-    line = mult[which // 16, pl.ds(which % 16, 1), :]
+    line = mult[which // 8, pl.ds(which % 8, 1), :]
     keep = lax.broadcasted_iota(jnp.int32, (1, ORBS), 1) == which
     diagonal = jnp.sum(jnp.where(keep, line, 0.0), axis=1, keepdims=True)
     denominator = 2.0 * coupling_z + 4.0 * coupling_xy + 1.0 + jnp.abs(diagonal)
@@ -313,8 +325,8 @@
                 psi.at[pl.ds(2 * to, 2), :, cols], cube.at[:, slab, cols],
                 y_send.at[chunk], y_recv.at[chunk], orb, to,
             ).start()
-    for step in range(1, BOX):
-        remote(pot, vfull.at[slab, :], v_sem.at[0], v_sem.at[1], orb, (box + step) % BOX).start()
+            if chunk == CHUNKS - 2:
+                remote(pot, vfull.at[slab, :], v_sem.at[0], v_sem.at[1], orb, to).start()
     pl.semaphore_wait(plane_sem, 7)
 
     def send_psi(step, carry):
@@ -335,7 +347,7 @@
             c_mine.wait()
         third = cube.at[:, pl.ds(0, 3 * DEPTH), pl.ds(chunk * width, width)]
         wait_for(third, y_recv.at[chunk])
-        if chunk == CHUNKS - 1:
+        if chunk == CHUNKS - 2:
             v_mine.wait()
             wait_for(vfull.at[pl.ds(0, 3 * DEPTH)], v_sem.at[1])
 
@@ -367,9 +379,11 @@
     pieces2 = pieces.reshape(SLOTS * ORB * 8, 128)
     applied2 = app_pieces.reshape(SLOTS * ORB * 8, 128)
     resid2 = resid.reshape(ORBS * 8, 128)
-    pick = (
-        lax.broadcasted_iota(jnp.int32, (ORBS, SLOTS * ORB), 1) == slots[...]
-    ).astype(F32).astype(BF16)
+    wanted = jnp.broadcast_to(slots[...].astype(F32), (ORBS, ORBS)).T
+    column = lax.broadcasted_iota(jnp.int32, (ORBS, ORBS), 1).astype(F32)
+    pick = jnp.concatenate(
+        [(column + float(k * ORBS) == wanted).astype(F32) for k in range(SLOTS * ORB // ORBS)], 1
+    ).astype(BF16)
 
     def choose(ref, hi, lo):
         for k in range(8):
@@ -387,44 +401,30 @@
 
     scale = 1.0 / float(G**3)
     total = dot_nt(c_hi[...], a_hi[...]) + dot_nt(c_lo[...], a_hi[...]) + dot_nt(c_hi[...], a_lo[...])
-    part[...] = (total * scale).reshape(16, 16, ORBS)
-
-    a_me = x * 4 + box
-    b_me = z * 2 + core
+    part[...] = (total * scale).reshape(32, 8, ORBS)
+
+    a_me = (x * 4 + box) * 2 + core
 
     def a_peer(step):
-        return ((x + step // 4) % 4) * 16 + z * 2 + core, (box + step % 4) % 4
-
-    def b_peer(step):
-        return x * 16 + ((z + step // 2) % 8) * 2 + (core + step % 2) % 2, box
-
-    def send_rows(step, carry):
+        to_orb = ((x + step // 8) % 4) * 16 + z * 2 + (core + step % 2) % 2
+        return to_orb, (box + (step // 2) % 4) % 4
+
+    for step in range(1, 32):
         to_orb, to_box = a_peer(step)
-        a_to = (to_orb // 16) * 4 + to_box
+        a_to = ((to_orb // 16) * 4 + to_box) * 2 + to_orb % 2
         remote(part.at[a_to], rs.at[a_me], r_sem.at[0], r_sem.at[1], to_orb, to_box).start()
-        return carry
-
-    lax.fori_loop(1, 16, send_rows, 0)
     rs[a_me] = part[a_me]
-    wait_for(rs.at[pl.ds(0, 15)], r_sem.at[1])
-    bb[b_me] = jnp.sum(rs[...], axis=0)
-
-    def send_sum(step, carry):
-        to_orb, to_box = b_peer(step)
-        remote(bb.at[b_me], bb.at[b_me], r_sem.at[2], r_sem.at[3], to_orb, to_box).start()
-        return carry
-
-    lax.fori_loop(1, 16, send_sum, 0)
-    wait_for(bb.at[pl.ds(0, 15)], r_sem.at[3])
+    wait_for(rs.at[pl.ds(0, 31)], r_sem.at[1])
+    bb[z] = jnp.sum(rs[...], axis=0)
+    for step in range(1, 8):
+        to_orb = x * 16 + ((z + step) % 8) * 2 + core
+        remote(bb.at[z], bb.at[z], r_sem.at[2], r_sem.at[3], to_orb, box).start()
+    wait_for(bb.at[pl.ds(0, 7)], r_sem.at[3])
     mult[a_me] = jnp.sum(bb[...], axis=0)
-
-    def send_total(step, carry):
+    for step in range(1, 32):
         to_orb, to_box = a_peer(step)
         remote(mult.at[a_me], mult.at[a_me], r_sem.at[4], r_sem.at[5], to_orb, to_box).start()
-        return carry
-
-    lax.fori_loop(1, 16, send_total, 0)
-    wait_for(mult.at[pl.ds(0, 15)], r_sem.at[5])
+    wait_for(mult.at[pl.ds(0, 31)], r_sem.at[5])
     m_hi, m_lo = split(mult[...].reshape(ORBS, ORBS).T)
     for k in range(8):
         lanes = pl.ds(k * 128, 128)
@@ -480,9 +480,9 @@
     wait_for(vfull.at[pl.ds(0, 3 * DEPTH)], v_sem.at[0])
     wait_for(pieces.at[pl.ds(0, SLOTS * (ORB - 1))], p_sem.at[0])
     wait_for(app_pieces.at[pl.ds(0, SLOTS * ORB - 2)], a_sem.at[0])
-    wait_for(part.at[pl.ds(0, 15)], r_sem.at[0])
-    wait_for(bb.at[pl.ds(0, 15)], r_sem.at[2])
-    wait_for(mult.at[pl.ds(0, 15)], r_sem.at[4])
+    wait_for(part.at[pl.ds(0, 31)], r_sem.at[0])
+    wait_for(bb.at[pl.ds(0, 7)], r_sem.at[2])
+    wait_for(mult.at[pl.ds(0, 31)], r_sem.at[4])
     wait_for(resid.at[pl.ds(0, OWN * (ORB - 1))], f_send)
     finish(OWN - 1, pair)
 
@@ -502,7 +502,7 @@
     padded = lambda pad: v16(TILES + 2 * pad, 2 * G, LANES)
     residual, direction, mult = pl.pallas_call(
         step_kernel,
-        out_shape=[shape(OWN, DEPTH, PLANE), shape(OWN, DEPTH, PLANE), shape(16, 16, ORBS)],
+        out_shape=[v32(OWN, DEPTH, PLANE), v32(OWN, DEPTH, PLANE), v32(32, 8, ORBS)],
         in_specs=[ANY, ANY, VMEM] + [ANY] * 5,
         out_specs=[VMEM] * 3,
         scratch_shapes=[
@@ -511,7 +511,7 @@
         ]
         + [v16(*t.shape) for t in consts]
         + [padded(KPAD)] * 2 + [padded(FPAD)] * 4 + [v32(TILES, 2 * G, LANES)]
-        + [v32(16, 16, ORBS)] * 3 + [v32(ORBS, 8, 128)]
+        + [v32(32, 8, ORBS)] * 2 + [v32(8, 8, ORBS)] + [v32(ORBS, 8, 128)]
         + [v16(ORBS, 1024)] * 4 + [v32(OWN, 32, PLANE)]
         + [
             DMA((8,)), DMA((CHUNKS,)), DMA((CHUNKS,)), DMA((2,)), DMA((2,)), DMA((2,)), DMA((6,)),
@@ -521,7 +521,7 @@
             has_side_effects=True, vmem_limit_bytes=VLIMIT, collective_id=0
         ),
         name="orbital_step",
-    )(psi, potential, orbital_slot.reshape(ORBS, 1), *consts)
+    )(psi, potential, orbital_slot.reshape(1, ORBS), *consts)
     return residual, direction, mult.reshape(ORBS, ORBS)
 
 

time: 183 us -> 172 us (0.940)
  Pallas kernels: 176 us -> 168 us
  local copies, waits for them, and re-layouts: 5.53 us -> 2.64 us
    pallas_call x1, Pallas kernels: 176 us -> 168 us  [local(): pl.pallas_call(step_kernel, out_shape=[v32(OWN, DEPTH, PLANE), v32(OWN, D...]
    unnamed x7 -> x3, local copies, waits for them, and re-layouts: 4.05 us -> 2.64 us
where the time goes in v3:
time: 172 us; the launch traced here: 171 us
  Pallas kernels  168 us (98%)
  local copies, waits for them, and re-layouts  2.64 us (2%)
    pallas_call x1, Pallas kernels, local(): pl.pallas_call(step_kernel, out_shape=[v32(OWN, DEPTH, PLANE), v32(OWN, D...  168 us

profile of v3, /device:TPU:2, one launch (start us, length us, event | category | flops | bytes accessed | tf_op | source)
XLA Modules:
  0.0 170.9 jit_solution(466317476129978859)
XLA Ops:
  0.6 167.6 %orbital_step.1 = (f32[4,16,4096]{2,1,0:T(8,128)S(1)}, f32[4,16,4096]{2,1,0:T(8,128)S(1)}, f32[32,8,256]{2,1,0:T(8,128)S(1)}) custom-call(f32[8,16,4096]{2,1,0:T(8,128)} %psi.1, f32[16,4096]{1,0:T(8,128)} %pot.1, s32[1,256]{1,0:T(1,128)} %bitcast.3, bf16[128,192]{1,0:T(8,128)(2,1)} %constant.10.clone.z_in_h, bf16[64,192]{1,0:T(8,128)(2,1)} %constant.11.clone.z_out_h, ...), custom_call_target="tpu_custom_call" | custom-call | tf_op jit(solution)/shard_map/orbital_step/pallas_call | solution.py:503
  168.3 1.0 copy.14
  169.2 0.7 copy.16
  170.0 1.0 copy.15

commit v4 on v3

--- a/solution.py
+++ b/solution.py
@@ -264,36 +264,62 @@
     return lax.dot_general(left, right, (((1,), (1,)), ((), ())), preferred_element_type=F32)
 
 
-def relax(resid, mult, which, box, resid_out, direct_out):
-    lane = lax.broadcasted_iota(jnp.int32, (32, PLANE), 1)
-    row = lax.broadcasted_iota(jnp.int32, (32, PLANE), 0)
-    inside = ((row >= 8) | (box > 0)) & ((row < 24) | (box < BOX - 1))
-    col = lane % G
-    line = mult[which // 8, pl.ds(which % 8, 1), :]
+def inverse_of(mult_t, which):
+    line = mult_t[which // 8, pl.ds(which % 8, 1), :]
     keep = lax.broadcasted_iota(jnp.int32, (1, ORBS), 1) == which
     diagonal = jnp.sum(jnp.where(keep, line, 0.0), axis=1, keepdims=True)
-    denominator = 2.0 * coupling_z + 4.0 * coupling_xy + 1.0 + jnp.abs(diagonal)
-    inverse = 1.0 / denominator
-    resid = jnp.where(inside, resid, 0.0)
-    resid_out[...] = resid[8:24]
-    now = resid * inverse
+    return 1.0 / (2.0 * coupling_z + 4.0 * coupling_xy + 1.0 + jnp.abs(diagonal))
+
+
+def relax(resid, inverse, box, direct_out):
+    lane = lax.broadcasted_iota(jnp.int32, (32, 128), 1)
+    row = lax.broadcasted_iota(jnp.int32, (32, 128), 0)
+    inside = ((row >= 8) | (box > 0)) & ((row < 24) | (box < BOX - 1))
+    factor = jnp.where(inside, jnp.broadcast_to(inverse, (32, 128)), 0.0)
+    first_col, last_col, first_row = lane % G == 0, lane % G == G - 1, lane < G
+    count = PLANE // 128
+    start = [jnp.where(inside, resid[:, k * 128 : (k + 1) * 128], 0.0) for k in range(count)]
+    now = [part * factor for part in start]
     for _ in range(SWEEPS):
-        side = jnp.where(col != 0, pltpu.roll(now, 1, 1), 0.0)
-        side = side + jnp.where(col != G - 1, pltpu.roll(now, PLANE - 1, 1), 0.0)
-        side = side + jnp.where(lane >= G, pltpu.roll(now, G, 1), 0.0)
-        side = side + jnp.where(lane < PLANE - G, pltpu.roll(now, PLANE - G, 1), 0.0)
-        along_z = pltpu.roll(now, 1, 0) + pltpu.roll(now, 31, 0)
-        now = jnp.where(inside, (resid + coupling_xy * side + coupling_z * along_z) * inverse, 0.0)
-    direct_out[...] = now[8:24]
+        turned = [pltpu.roll(part, G, 1) for part in now]
+        pairs = [turned[0]] + [turned[k - 1] + turned[k] for k in range(1, count)] + [turned[-1]]
+        following = []
+        for k in range(count):
+            side = jnp.where(first_row, pairs[k], pairs[k + 1])
+            side = side + jnp.where(first_col, 0.0, pltpu.roll(now[k], 1, 1))
+            side = side + jnp.where(last_col, 0.0, pltpu.roll(now[k], 127, 1))
+            along_z = pltpu.roll(now[k], 1, 0) + pltpu.roll(now[k], 31, 0)
+            following.append((start[k] + coupling_xy * side + coupling_z * along_z) * factor)
+        now = following
+    for k in range(count):
+        direct_out[:, k * 128 : (k + 1) * 128] = now[k][8:24]
+
+
+def finish_kernel(resid, direct, mult, ext, inverse, resid_out, direct_out, mult_out, last, sems):
+    box = lax.axis_index("box")
+    done = pl.ds(0, OWN - 1)
+    copies = [
+        pltpu.make_async_copy(direct, direct_out.at[done], sems.at[0]),
+        pltpu.make_async_copy(resid, resid_out.at[done], sems.at[1]),
+        pltpu.make_async_copy(ext.at[pl.ds(8, DEPTH)], resid_out.at[OWN - 1], sems.at[2]),
+        pltpu.make_async_copy(mult, mult_out, sems.at[3]),
+    ]
+    for copy in copies:
+        copy.start()
+    relax(ext[...], inverse[0:1, 0:1], box, last)
+    copies.append(pltpu.make_async_copy(last, direct_out.at[OWN - 1], sems.at[4]))
+    copies[-1].start()
+    for copy in copies:
+        copy.wait()
 
 
 def step_kernel(
     psi, pot, slots, z_in_h, z_out_h, into_h, back_h, kin_h,
-    resid_out, direct_out, mult,
+    resid_out, direct_out, mult_out, ext_out, inverse_out,
     pieces, app_pieces, cube, vfull, applied,
     z_in, z_out, into, back, kin,
     f_c_hi, f_c_lo, f_t_hi, f_t_lo, f_s_hi, f_s_lo, kz,
-    part, rs, bb, resid, c_hi, c_lo, a_hi, a_lo, ext,
+    part, rs, bb, mult, resid, c_hi, c_lo, a_hi, a_lo, a_sum, m_side, ext,
     own, y_send, y_recv, v_sem, p_sem, a_sem, r_sem, f_send, f_recv, h_send, h_recv, tab, plane_sem, all_sem,
 ):
     orb, box, x, z, core = place()
@@ -385,22 +411,25 @@
         [(column + float(k * ORBS) == wanted).astype(F32) for k in range(SLOTS * ORB // ORBS)], 1
     ).astype(BF16)
 
-    def choose(ref, hi, lo):
+    def choose(ref, hi, lo, both=None):
         for k in range(8):
             lanes = pl.ds(k * 128, 128)
             high, low = split(ref[pl.ds(k, SLOTS * ORB, stride=8), :])
-            hi[:, lanes] = mm(pick, high).astype(BF16)
-            lo[:, lanes] = mm(pick, low).astype(BF16)
+            high, low = mm(pick, high), mm(pick, low)
+            hi[:, lanes] = high.astype(BF16)
+            lo[:, lanes] = low.astype(BF16)
+            if both is not None:
+                both[pl.ds(k * ORBS, ORBS), :] = high + low
 
     p_mine.wait()
     wait_for(pieces.at[pl.ds(0, SLOTS * (ORB - 1))], p_sem.at[1])
     choose(pieces2, c_hi, c_lo)
     a_mine.wait()
     wait_for(app_pieces.at[pl.ds(0, SLOTS * ORB - 2)], a_sem.at[1])
-    choose(applied2, a_hi, a_lo)
+    choose(applied2, a_hi, a_lo, a_sum)
 
     scale = 1.0 / float(G**3)
-    total = dot_nt(c_hi[...], a_hi[...]) + dot_nt(c_lo[...], a_hi[...]) + dot_nt(c_hi[...], a_lo[...])
+    total = dot_nt(a_hi[...], c_hi[...]) + dot_nt(a_hi[...], c_lo[...]) + dot_nt(a_lo[...], c_hi[...])
     part[...] = (total * scale).reshape(32, 8, ORBS)
 
     a_me = (x * 4 + box) * 2 + core
@@ -425,17 +454,19 @@
         to_orb, to_box = a_peer(step)
         remote(mult.at[a_me], mult.at[a_me], r_sem.at[4], r_sem.at[5], to_orb, to_box).start()
     wait_for(mult.at[pl.ds(0, 31)], r_sem.at[5])
-    m_hi, m_lo = split(mult[...].reshape(ORBS, ORBS).T)
-    for k in range(8):
-        lanes = pl.ds(k * 128, 128)
-        fix = mm(m_hi, c_hi[:, lanes]) + mm(m_hi, c_lo[:, lanes]) + mm(m_lo, c_hi[:, lanes])
-        value = a_hi[:, lanes].astype(F32) + a_lo[:, lanes].astype(F32) - fix
-        resid2[pl.ds(k, ORBS, stride=8), :] = value
-
     z_rows = pl.ds(pl.multiple_of(8 + (orb // 32) * 8, 8), 8)
     lanes = pl.ds(pl.multiple_of((orb % 32) * 128, 128), 128)
     r_mine = []
+    mult2 = mult.reshape(ORBS, ORBS)
+    for h in range(2):
+        m_side[pl.ds(h * ORBS, ORBS), :] = mult2[:, pl.ds(h * 128, 128)]
     for n in range(OWN):
+        sides = [m_side[pl.ds(h * ORBS + n, ORB, stride=OWN), :] for h in range(2)]
+        m_hi, m_lo = split(jnp.concatenate(sides, 1))
+        fix = mm(m_hi, c_hi[...]) + mm(m_hi, c_lo[...]) + mm(m_lo, c_hi[...])
+        for k in range(8):
+            value = a_sum[pl.ds(k * ORBS + n, ORB, stride=OWN), :] - fix[:, k * 128 : (k + 1) * 128]
+            resid2[pl.ds(n * 8 + k, ORB, stride=OWN * 8), :] = value
         landing = ext.at[pl.ds(n, 1), z_rows, lanes]
         copy = pltpu.make_async_copy(resid.at[pl.ds(orb * OWN + n, 1)], landing, own.at[4 + n])
         copy.start()
@@ -465,8 +496,11 @@
     def finish(n, pair):
         for copy in pair:
             copy.wait()
-        relax(ext[n], mult, orb * OWN + n, box, resid_out.at[n], direct_out.at[n])
-
+        resid_out[n] = ext[n, 8:24, :]
+        relax(ext[n], inverse_of(mult, orb * OWN + n), box, direct_out.at[n])
+
+    mult_out[...] = mult2[...].T
+    inverse_out[...] = jnp.broadcast_to(inverse_of(mult, orb * OWN + OWN - 1), (8, 128))
     pair = None
     for n in range(OWN):
         r_mine[n].wait()
@@ -484,7 +518,9 @@
     wait_for(bb.at[pl.ds(0, 7)], r_sem.at[2])
     wait_for(mult.at[pl.ds(0, 31)], r_sem.at[4])
     wait_for(resid.at[pl.ds(0, OWN * (ORB - 1))], f_send)
-    finish(OWN - 1, pair)
+    for copy in pair:
+        copy.wait()
+    ext_out[...] = ext[OWN - 1]
 
 
 DMA = pltpu.SemaphoreType.DMA
@@ -500,19 +536,22 @@
     v32 = lambda *dims: pltpu.VMEM(dims, F32)
     v16 = lambda *dims: pltpu.VMEM(dims, BF16)
     padded = lambda pad: v16(TILES + 2 * pad, 2 * G, LANES)
-    residual, direction, mult = pl.pallas_call(
+    residual, direction, mult, ext, inverse = pl.pallas_call(
         step_kernel,
-        out_shape=[v32(OWN, DEPTH, PLANE), v32(OWN, DEPTH, PLANE), v32(32, 8, ORBS)],
+        out_shape=[
+            v32(OWN - 1, DEPTH, PLANE), v32(OWN - 1, DEPTH, PLANE), v32(ORBS, ORBS),
+            v32(32, PLANE), v32(8, 128),
+        ],
         in_specs=[ANY, ANY, VMEM] + [ANY] * 5,
-        out_specs=[VMEM] * 3,
+        out_specs=[VMEM] * 5,
         scratch_shapes=[
             v32(SLOTS * ORB, 8, 128), v32(SLOTS * ORB, 8, 128),
             v32(2, G, PLANE), v32(G, PLANE), v32(2, G, PLANE),
         ]
         + [v16(*t.shape) for t in consts]
         + [padded(KPAD)] * 2 + [padded(FPAD)] * 4 + [v32(TILES, 2 * G, LANES)]
-        + [v32(32, 8, ORBS)] * 2 + [v32(8, 8, ORBS)] + [v32(ORBS, 8, 128)]
-        + [v16(ORBS, 1024)] * 4 + [v32(OWN, 32, PLANE)]
+        + [v32(32, 8, ORBS)] * 2 + [v32(8, 8, ORBS)] + [v32(32, 8, ORBS)] + [v32(ORBS, 8, 128)]
+        + [v16(ORBS, 1024)] * 4 + [v32(8 * ORBS, 128), v32(2 * ORBS, 128)] + [v32(OWN, 32, PLANE)]
         + [
             DMA((8,)), DMA((CHUNKS,)), DMA((CHUNKS,)), DMA((2,)), DMA((2,)), DMA((2,)), DMA((6,)),
             DMA, DMA((OWN,)), DMA((2 * OWN,)), DMA((2 * OWN,)), DMA((5,)), REGULAR, REGULAR,
@@ -522,7 +561,15 @@
         ),
         name="orbital_step",
     )(psi, potential, orbital_slot.reshape(1, ORBS), *consts)
-    return residual, direction, mult.reshape(ORBS, ORBS)
+    return pl.pallas_call(
+        finish_kernel,
+        out_shape=[shape(OWN, DEPTH, PLANE), shape(OWN, DEPTH, PLANE), shape(ORBS, ORBS)],
+        in_specs=[VMEM] * 5,
+        out_specs=[ANY] * 3,
+        scratch_shapes=[v32(DEPTH, PLANE), DMA((5,))],
+        compiler_params=pltpu.CompilerParams(vmem_limit_bytes=16 * 2**20),
+        name="last_orbital",
+    )(residual, direction, mult, ext, inverse)
 
 
 def solution(mesh):

time: 172 us -> 169 us (0.983)
  local copies, waits for them, and re-layouts: 2.64 us -> 0 us
    unnamed x3 -> x0, local copies, waits for them, and re-layouts: 2.64 us -> none
    pallas_call x1 -> x2, Pallas kernels: 168 us -> 167 us  [the longest x1 165 us: local(): pl.pallas_call(step_kernel, out_shape=[v32(OWN - 1, DEPTH, PLANE), v32(OW...]
where the time goes in v4:
time: 169 us; the launch traced here: 168 us
  Pallas kernels  167 us (99%)
    pallas_call x1, Pallas kernels, local(): pl.pallas_call(step_kernel, out_shape=[v32(OWN - 1, DEPTH, PLANE), v32(OW...  165 us

profile of v4, /device:TPU:2, one launch (start us, length us, event | category | flops | bytes accessed | tf_op | source)
XLA Modules:
  0.0 167.9 jit_solution(817398673057177678)
XLA Ops:
  0.6 164.8 %orbital_step.1 = (f32[3,16,4096]{2,1,0:T(8,128)S(1)}, f32[3,16,4096]{2,1,0:T(8,128)S(1)}, f32[256,256]{1,0:T(8,128)S(1)}, f32[32,4096]{1,0:T(8,128)S(1)}, f32[8,128]{1,0:T(8,128)S(1)}) custom-call(f32[8,16,4096]{2,1,0:T(8,128)} %psi.1, f32[16,4096]{1,0:T(8,128)} %pot.1, s32[1,256]{1,0:T(1,128)} %bitcast.1, bf16[128,192]{1,0:T(8,128)(2,1)} %constant.10.clone.z_in_h, ...), custom_call_target="tpu_custom_call" | custom-call | tf_op jit(solution)/shard_map/orbital_step/pallas_call | solution.py:539
  165.4 2.4 %last_orbital.1 = (f32[4,16,4096]{2,1,0:T(8,128)}, f32[4,16,4096]{2,1,0:T(8,128)}, f32[256,256]{1,0:T(8,128)}) custom-call(f32[3,16,4096]{2,1,0:T(8,128)S(1)} %get-tuple-element.8.resid, f32[3,16,4096]{2,1,0:T(8,128)S(1)} %get-tuple-element.9.direct, f32[256,256]{1,0:T(8,128)S(1)} %get-tuple-element.10.mult, f32[32,4096]{1,0:T(8,128)S(1)} %get-tuple-element.11.ext, ...), custom_call_target="tpu_custom_call" | custom-call | tf_op jit(solution)/shard_map/last_orbital/pallas_call | solution.py:564

commit v5 on v4

--- a/solution.py
+++ b/solution.py
@@ -148,9 +148,10 @@
 
 
 CHUNKS = 4
-
-
-def greet(orb, box, x, z, core, plane_sem):
+GROUPS = ((0, 2), (2, 1), (3, 1))
+
+
+def greet(orb, box, x, z, core, plane_sem, meanwhile):
     barrier = pltpu.get_barrier_semaphore()
 
     def signal(sem, to_orb, to_box):
@@ -173,9 +174,10 @@
         for step in range(1, BOX):
             signal(sem, orb, (box + step) % BOX)
 
-    beside(barrier)
     lax.fori_loop(1, 8, along_z, 0)
     lax.fori_loop(1, 8, across(barrier), 0)
+    beside(barrier)
+    meanwhile()
     pl.semaphore_wait(barrier, 7 + 7 + 3)
     lax.fori_loop(1, 8, across(plane_sem), 0)
     return beside
@@ -329,20 +331,19 @@
             ((z_in_h, z_in), (z_out_h, z_out), (into_h, into), (back_h, back), (kin_h, kin))
         )
     ]
-    for copy in table_copies:
-        copy.start()
     slab = pl.ds(pl.multiple_of(box * DEPTH, DEPTH), DEPTH)
     width = PLANE // CHUNKS
     v_mine = pltpu.make_async_copy(pot, vfull.at[slab, :], own.at[0])
-    v_mine.start()
     target = pl.ds(pl.multiple_of(orb * SLOTS, SLOTS), SLOTS)
     z_rows, lanes = tile_of(orb)
     p_mine = pltpu.make_async_copy(psi.at[:, z_rows, lanes], pieces.at[target], own.at[1])
-    p_mine.start()
     c_mine = pltpu.make_async_copy(psi.at[pl.ds(2 * box, 2)], cube.at[:, slab, :], own.at[2])
-    c_mine.start()
-
-    beside = greet(orb, box, x, z, core, plane_sem)
+
+    def meanwhile():
+        for copy in [*table_copies, v_mine, p_mine, c_mine]:
+            copy.start()
+
+    beside = greet(orb, box, x, z, core, plane_sem, meanwhile)
     for chunk in range(CHUNKS):
         cols = pl.ds(chunk * width, width)
         for step in range(1, BOX):
@@ -460,54 +461,64 @@
     mult2 = mult.reshape(ORBS, ORBS)
     for h in range(2):
         m_side[pl.ds(h * ORBS, ORBS), :] = mult2[:, pl.ds(h * 128, 128)]
-    for n in range(OWN):
-        sides = [m_side[pl.ds(h * ORBS + n, ORB, stride=OWN), :] for h in range(2)]
+    for g, (first, count) in enumerate(GROUPS):
+        members = range(first, first + count)
+        sides = [
+            jnp.concatenate([m_side[pl.ds(h * ORBS + n, ORB, stride=OWN), :] for n in members], 0)
+            for h in range(2)
+        ]
         m_hi, m_lo = split(jnp.concatenate(sides, 1))
         fix = mm(m_hi, c_hi[...]) + mm(m_hi, c_lo[...]) + mm(m_lo, c_hi[...])
-        for k in range(8):
-            value = a_sum[pl.ds(k * ORBS + n, ORB, stride=OWN), :] - fix[:, k * 128 : (k + 1) * 128]
-            resid2[pl.ds(n * 8 + k, ORB, stride=OWN * 8), :] = value
-        landing = ext.at[pl.ds(n, 1), z_rows, lanes]
-        copy = pltpu.make_async_copy(resid.at[pl.ds(orb * OWN + n, 1)], landing, own.at[4 + n])
+        for i, n in enumerate(members):
+            for k in range(8):
+                part_fix = fix[i * ORB : (i + 1) * ORB, k * 128 : (k + 1) * 128]
+                value = a_sum[pl.ds(k * ORBS + n, ORB, stride=OWN), :] - part_fix
+                resid2[pl.ds(n * 8 + k, ORB, stride=OWN * 8), :] = value
+        landing = ext.at[pl.ds(first, count), z_rows, lanes]
+        copy = pltpu.make_async_copy(resid.at[pl.ds(orb * OWN + first, count)], landing, own.at[4 + g])
         copy.start()
         r_mine.append(copy)
 
-        def send_resid(step, carry, n=n, landing=landing):
+        def send_resid(step, carry, g=g, first=first, count=count, landing=landing):
             to = shifted(orb, step)
-            remote(resid.at[pl.ds(to * OWN + n, 1)], landing, f_send, f_recv.at[n], to, box).start()
+            remote(
+                resid.at[pl.ds(to * OWN + first, count)], landing, f_send, f_recv.at[g], to, box
+            ).start()
             return carry
 
         lax.fori_loop(1, ORB, send_resid, 0)
 
-    def halo(n):
-        one = pl.ds(n, 1)
+    def halo(g):
+        r_mine[g].wait()
+        first, count = GROUPS[g]
+        wait_for(resid.at[pl.ds(0, count * (ORB - 1))], f_recv.at[g])
+        some = pl.ds(first, count)
         up = remote(
-            ext.at[one, pl.ds(20, 4), :], ext.at[one, pl.ds(4, 4), :],
-            h_send.at[2 * n], h_recv.at[2 * n], orb, (box + 1) % BOX,
+            ext.at[some, pl.ds(20, 4), :], ext.at[some, pl.ds(4, 4), :],
+            h_send.at[2 * g], h_recv.at[2 * g], orb, (box + 1) % BOX,
         )
         down = remote(
-            ext.at[one, pl.ds(8, 4), :], ext.at[one, pl.ds(24, 4), :],
-            h_send.at[2 * n + 1], h_recv.at[2 * n + 1], orb, (box + 3) % BOX,
+            ext.at[some, pl.ds(8, 4), :], ext.at[some, pl.ds(24, 4), :],
+            h_send.at[2 * g + 1], h_recv.at[2 * g + 1], orb, (box + 3) % BOX,
         )
         up.start()
         down.start()
         return up, down
 
-    def finish(n, pair):
+    def finish(g, pair):
         for copy in pair:
             copy.wait()
-        resid_out[n] = ext[n, 8:24, :]
-        relax(ext[n], inverse_of(mult, orb * OWN + n), box, direct_out.at[n])
+        first, count = GROUPS[g]
+        for n in range(first, first + count):
+            resid_out[n] = ext[n, 8:24, :]
+            relax(ext[n], inverse_of(mult, orb * OWN + n), box, direct_out.at[n])
 
     mult_out[...] = mult2[...].T
     inverse_out[...] = jnp.broadcast_to(inverse_of(mult, orb * OWN + OWN - 1), (8, 128))
-    pair = None
-    for n in range(OWN):
-        r_mine[n].wait()
-        wait_for(resid.at[pl.ds(0, ORB - 1)], f_recv.at[n])
-        following = halo(n)
-        if pair is not None:
-            finish(n - 1, pair)
+    pair = halo(0)
+    for g in range(1, len(GROUPS)):
+        following = halo(g)
+        finish(g - 1, pair)
         pair = following
     for chunk in range(CHUNKS):
         wait_for(cube.at[:, pl.ds(0, 3 * DEPTH), pl.ds(chunk * width, width)], y_send.at[chunk])

time: 169 us -> 169 us (level)
  no operation moved by 1% of the time
where the time goes in v5:
time: 169 us; the launch traced here: 168 us
  Pallas kernels  167 us (99%)
    pallas_call x1, Pallas kernels, local(): pl.pallas_call(step_kernel, out_shape=[v32(OWN - 1, DEPTH, PLANE), v32(OW...  164 us

profile of v5, /device:TPU:2, one launch (start us, length us, event | category | flops | bytes accessed | tf_op | source)
XLA Modules:
  0.0 167.6 jit_solution(6351724851543230998)
XLA Ops:
  0.6 164.4 %orbital_step.1 = (f32[3,16,4096]{2,1,0:T(8,128)S(1)}, f32[3,16,4096]{2,1,0:T(8,128)S(1)}, f32[256,256]{1,0:T(8,128)S(1)}, f32[32,4096]{1,0:T(8,128)S(1)}, f32[8,128]{1,0:T(8,128)S(1)}) custom-call(f32[8,16,4096]{2,1,0:T(8,128)} %psi.1, f32[16,4096]{1,0:T(8,128)} %pot.1, s32[1,256]{1,0:T(1,128)} %bitcast.1, bf16[128,192]{1,0:T(8,128)(2,1)} %constant.10.clone.z_in_h, ...), custom_call_target="tpu_custom_call" | custom-call | tf_op jit(solution)/shard_map/orbital_step/pallas_call | solution.py:550
  165.1 2.4 %last_orbital.1 = (f32[4,16,4096]{2,1,0:T(8,128)}, f32[4,16,4096]{2,1,0:T(8,128)}, f32[256,256]{1,0:T(8,128)}) custom-call(f32[3,16,4096]{2,1,0:T(8,128)S(1)} %get-tuple-element.8.resid, f32[3,16,4096]{2,1,0:T(8,128)S(1)} %get-tuple-element.9.direct, f32[256,256]{1,0:T(8,128)S(1)} %get-tuple-element.10.mult, f32[32,4096]{1,0:T(8,128)S(1)} %get-tuple-element.11.ext, ...), custom_call_target="tpu_custom_call" | custom-call | tf_op jit(solution)/shard_map/last_orbital/pallas_call | solution.py:575

commit v6 on v5

--- a/solution.py
+++ b/solution.py
@@ -183,7 +183,7 @@
     return beside
 
 
-def filters(cube, vfull, z_in, z_out, into, back, kin, out, c_hi, c_lo, t_hi, t_lo, s_hi, s_lo, kz, arrived, tabled):
+def filters(cube, vfull, z_in, z_out, into, back, kin, out, c_hi, c_lo, t_hi, t_lo, s_hi, s_lo, kz, arrived, tabled, ready, order, leave):
     for buf, pad in ((c_hi, KPAD), (c_lo, KPAD), (t_hi, FPAD), (t_lo, FPAD), (s_hi, FPAD), (s_lo, FPAD)):
         edge = jnp.zeros((pad, 2 * G, LANES), BF16)
         buf[pl.ds(0, pad)] = edge
@@ -249,7 +249,7 @@
     lax.fori_loop(early, TILES // group, kinetic, 0)
 
     def last(i, carry):
-        first = i * group
+        first = order(i) * group
         acc = kz[pl.ds(first, group)].reshape(group * 2 * G, LANES)
         acc = spread(s_hi, s_lo, back, 2 * FPAD + 1, first, acc)
         for j in range(group):
@@ -257,8 +257,10 @@
             for s in range(2):
                 low_row = (j * 2 + s) * G
                 out[s, :, lanes] = acc[low_row : low_row + G]
+        leave(first)
         return carry
 
+    ready()
     lax.fori_loop(0, TILES // group, last, 0)
 
 
@@ -378,30 +380,39 @@
             v_mine.wait()
             wait_for(vfull.at[pl.ds(0, 3 * DEPTH)], v_sem.at[1])
 
-    filters(
-        cube, vfull, z_in, z_out, into, back, kin, applied,
-        f_c_hi, f_c_lo, f_t_hi, f_t_lo, f_s_hi, f_s_lo, kz, arrived, tabled,
-    )
-    pl.semaphore_wait(all_sem, BOX - 1)
-
     a_target = pl.ds(orb * SLOTS + 2 * box, 2)
 
     def source(to_orb, to_box):
         z_rows = pl.ds(pl.multiple_of(to_box * DEPTH + (to_orb // 32) * 8, 8), 8)
         return applied.at[:, z_rows, pl.ds(pl.multiple_of((to_orb % 32) * 128, 128), 128)]
 
+    def ready():
+        pl.semaphore_wait(all_sem, BOX - 1)
+
+    def order(i):
+        return (z // 2 + (1 + i) * (1 + 2 * core)) % 4 + 4 * ((i // 4 + x) % 2)
+
+    def leave(first):
+        def send_applied(step, carry):
+            to_orb = ((step // BOX) % 2) * 32 + 2 * first + step // (2 * BOX)
+            to_box = (box + step % BOX) % BOX
+
+            @pl.when((to_orb != orb) | (to_box != box))
+            def _():
+                remote(
+                    source(to_orb, to_box), app_pieces.at[a_target], a_sem.at[0], a_sem.at[1], to_orb, to_box
+                ).start()
+
+            return carry
+
+        lax.fori_loop(0, 8 * BOX, send_applied, 0)
+
+    filters(
+        cube, vfull, z_in, z_out, into, back, kin, applied,
+        f_c_hi, f_c_lo, f_t_hi, f_t_lo, f_s_hi, f_s_lo, kz, arrived, tabled, ready, order, leave,
+    )
     a_mine = pltpu.make_async_copy(source(orb, box), app_pieces.at[a_target], own.at[3])
     a_mine.start()
-
-    def send_applied(step, carry):
-        to_orb = shifted(orb, step // BOX)
-        to_box = (box + step % BOX) % BOX
-        remote(
-            source(to_orb, to_box), app_pieces.at[a_target], a_sem.at[0], a_sem.at[1], to_orb, to_box
-        ).start()
-        return carry
-
-    lax.fori_loop(1, ORB * BOX, send_applied, 0)
 
     pieces2 = pieces.reshape(SLOTS * ORB * 8, 128)
     applied2 = app_pieces.reshape(SLOTS * ORB * 8, 128)

time: 169 us -> 164 us (0.970)
  Pallas kernels: 167 us -> 161 us
    pallas_call x1, Pallas kernels: 164 us -> 159 us  [local(): pl.pallas_call(step_kernel, out_shape=[v32(OWN - 1, DEPTH, PLANE), v32(OW...]
where the time goes in v6:
time: 164 us; the launch traced here: 162 us
  Pallas kernels  161 us (98%)
    pallas_call x1, Pallas kernels, local(): pl.pallas_call(step_kernel, out_shape=[v32(OWN - 1, DEPTH, PLANE), v32(OW...  159 us

profile of v6, /device:TPU:2, one launch (start us, length us, event | category | flops | bytes accessed | tf_op | source)
XLA Modules:
  0.0 162.2 jit_solution(16613304494188988215)
XLA Ops:
  0.6 159.1 %orbital_step.1 = (f32[3,16,4096]{2,1,0:T(8,128)S(1)}, f32[3,16,4096]{2,1,0:T(8,128)S(1)}, f32[256,256]{1,0:T(8,128)S(1)}, f32[32,4096]{1,0:T(8,128)S(1)}, f32[8,128]{1,0:T(8,128)S(1)}) custom-call(f32[8,16,4096]{2,1,0:T(8,128)} %psi.1, f32[16,4096]{1,0:T(8,128)} %pot.1, s32[1,256]{1,0:T(1,128)} %bitcast.1, bf16[128,192]{1,0:T(8,128)(2,1)} %constant.10.clone.z_in_h, ...), custom_call_target="tpu_custom_call" | custom-call | tf_op jit(solution)/shard_map/orbital_step/pallas_call | solution.py:561
  159.7 2.4 %last_orbital.1 = (f32[4,16,4096]{2,1,0:T(8,128)}, f32[4,16,4096]{2,1,0:T(8,128)}, f32[256,256]{1,0:T(8,128)}) custom-call(f32[3,16,4096]{2,1,0:T(8,128)S(1)} %get-tuple-element.8.resid, f32[3,16,4096]{2,1,0:T(8,128)S(1)} %get-tuple-element.9.direct, f32[256,256]{1,0:T(8,128)S(1)} %get-tuple-element.10.mult, f32[32,4096]{1,0:T(8,128)S(1)} %get-tuple-element.11.ext, ...), custom_call_target="tpu_custom_call" | custom-call | tf_op jit(solution)/shard_map/last_orbital/pallas_call | solution.py:586

commit v7 on v6

--- a/solution.py
+++ b/solution.py
@@ -123,7 +123,8 @@
 def shifted(orb, step):
     x, z, core = orb // 16, (orb // 2) % 8, orb % 2
     dx, dz, dc = step // 16, (step // 2) % 8, step % 2
-    return ((x + dx) % 4) * 16 + ((z + dz) % 8) * 2 + (core + dc) % 2
+    x, z = (x + dx * (1 + 2 * core)) % 4, (z + dz * (1 + 6 * core)) % 8
+    return x * 16 + z * 2 + (core + dc) % 2
 
 
 def remote(src, dst, send, recv, orb, box):
@@ -346,6 +347,14 @@
             copy.start()
 
     beside = greet(orb, box, x, z, core, plane_sem, meanwhile)
+
+    def send_psi(step, carry):
+        to = shifted(orb, step)
+        z_rows, lanes = tile_of(to)
+        remote(psi.at[:, z_rows, lanes], pieces.at[target], p_sem.at[0], p_sem.at[1], to, box).start()
+        return carry
+
+    lax.fori_loop(1, 8, lambda step, carry: send_psi(2 * step, carry), 0)
     for chunk in range(CHUNKS):
         cols = pl.ds(chunk * width, width)
         for step in range(1, BOX):
@@ -358,13 +367,11 @@
                 remote(pot, vfull.at[slab, :], v_sem.at[0], v_sem.at[1], orb, to).start()
     pl.semaphore_wait(plane_sem, 7)
 
-    def send_psi(step, carry):
-        to = shifted(orb, step)
-        z_rows, lanes = tile_of(to)
-        remote(psi.at[:, z_rows, lanes], pieces.at[target], p_sem.at[0], p_sem.at[1], to, box).start()
-        return carry
-
-    lax.fori_loop(1, ORB, send_psi, 0)
+    def send_far(i, carry):
+        apart = 1 + i // 8
+        return send_psi((apart // 2) * 16 + (i % 8) * 2 + apart % 2, carry)
+
+    lax.fori_loop(0, ORB - 8, send_far, 0)
     beside(all_sem)
 
     def tabled():

time: 164 us -> 164 us (level)
  no operation moved by 1% of the time
where the time goes in v7:
time: 164 us; the launch traced here: 163 us
  Pallas kernels  162 us (99%)
    pallas_call x1, Pallas kernels, local(): pl.pallas_call(step_kernel, out_shape=[v32(OWN - 1, DEPTH, PLANE), v32(OW...  159 us

profile of v7, /device:TPU:2, one launch (start us, length us, event | category | flops | bytes accessed | tf_op | source)
XLA Modules:
  0.0 162.5 jit_solution(13409800004073871651)
XLA Ops:
  0.6 159.4 %orbital_step.1 = (f32[3,16,4096]{2,1,0:T(8,128)S(1)}, f32[3,16,4096]{2,1,0:T(8,128)S(1)}, f32[256,256]{1,0:T(8,128)S(1)}, f32[32,4096]{1,0:T(8,128)S(1)}, f32[8,128]{1,0:T(8,128)S(1)}) custom-call(f32[8,16,4096]{2,1,0:T(8,128)} %psi.1, f32[16,4096]{1,0:T(8,128)} %pot.1, s32[1,256]{1,0:T(1,128)} %bitcast.1, bf16[128,192]{1,0:T(8,128)(2,1)} %constant.10.clone.z_in_h, ...), custom_call_target="tpu_custom_call" | custom-call | tf_op jit(solution)/shard_map/orbital_step/pallas_call | solution.py:568
  160.0 2.4 %last_orbital.1 = (f32[4,16,4096]{2,1,0:T(8,128)}, f32[4,16,4096]{2,1,0:T(8,128)}, f32[256,256]{1,0:T(8,128)}) custom-call(f32[3,16,4096]{2,1,0:T(8,128)S(1)} %get-tuple-element.8.resid, f32[3,16,4096]{2,1,0:T(8,128)S(1)} %get-tuple-element.9.direct, f32[256,256]{1,0:T(8,128)S(1)} %get-tuple-element.10.mult, f32[32,4096]{1,0:T(8,128)S(1)} %get-tuple-element.11.ext, ...), custom_call_target="tpu_custom_call" | custom-call | tf_op jit(solution)/shard_map/last_orbital/pallas_call | solution.py:593

commit v8 on v6

--- a/solution.py
+++ b/solution.py
@@ -262,10 +262,6 @@
 
     ready()
     lax.fori_loop(0, TILES // group, last, 0)
-
-
-def dot_nt(left, right):
-    return lax.dot_general(left, right, (((1,), (1,)), ((), ())), preferred_element_type=F32)
 
 
 def inverse_of(mult_t, which):
@@ -323,7 +319,7 @@
     pieces, app_pieces, cube, vfull, applied,
     z_in, z_out, into, back, kin,
     f_c_hi, f_c_lo, f_t_hi, f_t_lo, f_s_hi, f_s_lo, kz,
-    part, rs, bb, mult, resid, c_hi, c_lo, a_hi, a_lo, a_sum, m_side, ext,
+    part, rs, bb, mult, resid, c_hi, c_lo, a_hi, a_lo, a_sum, m_side, c_turned, ext,
     own, y_send, y_recv, v_sem, p_sem, a_sem, r_sem, f_send, f_recv, h_send, h_recv, tab, plane_sem, all_sem,
 ):
     orb, box, x, z, core = place()
@@ -423,25 +419,29 @@
         [(column + float(k * ORBS) == wanted).astype(F32) for k in range(SLOTS * ORB // ORBS)], 1
     ).astype(BF16)
 
-    def choose(ref, hi, lo, both=None):
+    def choose(ref, hi, lo, both=None, turned=None):
         for k in range(8):
             lanes = pl.ds(k * 128, 128)
             high, low = split(ref[pl.ds(k, SLOTS * ORB, stride=8), :])
-            high, low = mm(pick, high), mm(pick, low)
+            picked = mm(pick, jnp.concatenate([high, low], 1))
+            high, low = picked[:, :128], picked[:, 128:]
             hi[:, lanes] = high.astype(BF16)
             lo[:, lanes] = low.astype(BF16)
+            if turned is not None:
+                turned[0, lanes, :] = high.T.astype(BF16)
+                turned[1, lanes, :] = low.T.astype(BF16)
             if both is not None:
                 both[pl.ds(k * ORBS, ORBS), :] = high + low
 
     p_mine.wait()
     wait_for(pieces.at[pl.ds(0, SLOTS * (ORB - 1))], p_sem.at[1])
-    choose(pieces2, c_hi, c_lo)
+    choose(pieces2, c_hi, c_lo, turned=c_turned)
     a_mine.wait()
     wait_for(app_pieces.at[pl.ds(0, SLOTS * ORB - 2)], a_sem.at[1])
     choose(applied2, a_hi, a_lo, a_sum)
 
     scale = 1.0 / float(G**3)
-    total = dot_nt(a_hi[...], c_hi[...]) + dot_nt(a_hi[...], c_lo[...]) + dot_nt(a_lo[...], c_hi[...])
+    total = mm(a_hi[...], c_turned[0]) + mm(a_hi[...], c_turned[1]) + mm(a_lo[...], c_turned[0])
     part[...] = (total * scale).reshape(32, 8, ORBS)
 
     a_me = (x * 4 + box) * 2 + core
@@ -573,7 +573,7 @@
         + [v16(*t.shape) for t in consts]
         + [padded(KPAD)] * 2 + [padded(FPAD)] * 4 + [v32(TILES, 2 * G, LANES)]
         + [v32(32, 8, ORBS)] * 2 + [v32(8, 8, ORBS)] + [v32(32, 8, ORBS)] + [v32(ORBS, 8, 128)]
-        + [v16(ORBS, 1024)] * 4 + [v32(8 * ORBS, 128), v32(2 * ORBS, 128)] + [v32(OWN, 32, PLANE)]
+        + [v16(ORBS, 1024)] * 4 + [v32(8 * ORBS, 128), v32(2 * ORBS, 128), v16(2, 1024, ORBS)] + [v32(OWN, 32, PLANE)]
         + [
             DMA((8,)), DMA((CHUNKS,)), DMA((CHUNKS,)), DMA((2,)), DMA((2,)), DMA((2,)), DMA((6,)),
             DMA, DMA((OWN,)), DMA((2 * OWN,)), DMA((2 * OWN,)), DMA((5,)), REGULAR, REGULAR,

time: 164 us -> 163 us (level)
  no operation moved by 1% of the time
where the time goes in v8:
time: 163 us; the launch traced here: 161 us
  Pallas kernels  161 us (99%)
    pallas_call x1, Pallas kernels, local(): pl.pallas_call(step_kernel, out_shape=[v32(OWN - 1, DEPTH, PLANE), v32(OW...  158 us

profile of v8, /device:TPU:2, one launch (start us, length us, event | category | flops | bytes accessed | tf_op | source)
XLA Modules:
  0.0 161.4 jit_solution(18331590948718770268)
XLA Ops:
  0.6 158.2 %orbital_step.1 = (f32[3,16,4096]{2,1,0:T(8,128)S(1)}, f32[3,16,4096]{2,1,0:T(8,128)S(1)}, f32[256,256]{1,0:T(8,128)S(1)}, f32[32,4096]{1,0:T(8,128)S(1)}, f32[8,128]{1,0:T(8,128)S(1)}) custom-call(f32[8,16,4096]{2,1,0:T(8,128)} %psi.1, f32[16,4096]{1,0:T(8,128)} %pot.1, s32[1,256]{1,0:T(1,128)} %bitcast.1, bf16[128,192]{1,0:T(8,128)(2,1)} %constant.10.clone.z_in_h, ...), custom_call_target="tpu_custom_call" | custom-call | tf_op jit(solution)/shard_map/orbital_step/pallas_call | solution.py:561
  158.9 2.4 %last_orbital.1 = (f32[4,16,4096]{2,1,0:T(8,128)}, f32[4,16,4096]{2,1,0:T(8,128)}, f32[256,256]{1,0:T(8,128)}) custom-call(f32[3,16,4096]{2,1,0:T(8,128)S(1)} %get-tuple-element.8.resid, f32[3,16,4096]{2,1,0:T(8,128)S(1)} %get-tuple-element.9.direct, f32[256,256]{1,0:T(8,128)S(1)} %get-tuple-element.10.mult, f32[32,4096]{1,0:T(8,128)S(1)} %get-tuple-element.11.ext, ...), custom_call_target="tpu_custom_call" | custom-call | tf_op jit(solution)/shard_map/last_orbital/pallas_call | solution.py:586
